TPU v7x, 32 devices: a whole 2x2x4 slice. The times are simulated.
32 devices in a mesh: space: 8 (over y, x, core), tm: 2 (over z_hi), op: 2 (over z_lo).
Axes of the slice: x: 2, y: 2, z: 4 (z_hi: 2, z_lo: 2; z = z_hi * 2 + z_lo), core: 2. Of those that a mesh axis runs over, the one named last changes fastest.
Arguments:
- eigvecs: bfloat16 [2, 2, 256, 3, 16, 256], P('tm', None, None, None, 'space'), may hold values from -6 to 6
- links: float32 [2, 3, 3, 3, 2, 16, 256], P('tm', None, None, None, None, 'space'), may hold values from -2.5 to 2.5
- momenta: int32 [4, 3], P('op'), may hold values from -2 to 2
- coef_num: int32 [4, 4, 3], P(None, 'op'), may hold values from -3 to 3
- coef_den: int32 [4], replicated, may hold values from 1 to 6
- peram: bfloat16 [2, 256, 4, 4, 2, 256], P('tm'), may hold values from -0.25 to 0.25
Outputs:
- quark_lines: float32 [2, 4, 4, 4, 2, 256, 256], P('tm', 'op', None, None, None, 'space')
All inputs are finite; a program needn't handle non-finite values.
Results may differ from a plain program's by a relative error of at most 0.0053.
Values may be sent and summed in bfloat16 or wider, within the bound.
No kernel may reach another device: no remote copies, remote signals or barrier semaphores. Data moves between devices by JAX's collectives and lax.ppermute only.
A program may use at most 128 MiB of HBM per device.

v0:
```python
import functools
import math

import jax
import jax.numpy as jnp
from jax import lax
from jax.experimental import pallas as pl
from jax.experimental.pallas import tpu as pltpu
from jax.sharding import PartitionSpec as P

LY = 32
LZ = 8
NDIR = 3
SPINS = 16
ROWS = 16
HALF = 128


def from_behind(value, axis, steps):
    count = lax.axis_size(axis)
    pairs = [(source, (source + steps) % count) for source in range(count)]
    return lax.ppermute(value, axis, pairs)


def dot_nt(left, right):
    return lax.dot_general(
        left, right, (((1,), (1,)), ((), ())), preferred_element_type=jnp.float32
    )


def shift_y(arr):
    return pltpu.roll(arr, arr.shape[1] - LZ, 1)


def shift_z(arr):
    width = arr.shape[1]
    lane = lax.broadcasted_iota(jnp.int32, arr.shape, 1)
    near = pltpu.roll(arr, width - 1, 1)
    far = pltpu.roll(arr, LZ - 1, 1)
    return jnp.where((lane & (LZ - 1)) == LZ - 1, far, near)


def weighted_links(u_ref, phi_ref, shifted, dirs, plane, n_h, store):
    width = u_ref.shape[-1]
    for half in range(width // HALF):
        lanes = pl.ds(half * HALF, HALF)
        for col in range(3):
            acc = {}
            for slot, direc in enumerate(dirs):
                f_r = None
                f_i = None
                for col_two in range(3):
                    u_r = u_ref[direc, col, col_two, 0, pl.ds(plane, 1), lanes]
                    u_i = u_ref[direc, col, col_two, 1, pl.ds(plane, 1), lanes]
                    v_r = shifted[slot, 0, col_two, :, lanes]
                    v_i = shifted[slot, 1, col_two, :, lanes]
                    term_r = u_r * v_r - u_i * v_i
                    term_i = u_r * v_i + u_i * v_r
                    f_r = term_r if f_r is None else f_r + term_r
                    f_i = term_i if f_i is None else f_i + term_i
                for kind in range(2):
                    for hel in range(n_h):
                        p_r = phi_ref[kind, hel, direc, 0, pl.ds(plane, 1), lanes]
                        p_i = phi_ref[kind, hel, direc, 1, pl.ds(plane, 1), lanes]
                        g_r = p_r * f_r - p_i * f_i
                        g_i = p_r * f_i + p_i * f_r
                        if (kind, hel) in acc:
                            old_r, old_i = acc[kind, hel]
                            g_r, g_i = old_r + g_r, old_i + g_i
                        acc[kind, hel] = (g_r, g_i)
            for (kind, hel), both in acc.items():
                for part in range(2):
                    store(kind, hel, part, col, half, both[part].astype(jnp.bfloat16))


def products(mat, g_ref, h_ref, hel):
    n_b = mat.shape[0] // 2
    one = dot_nt(mat, g_ref[hel])
    two = dot_nt(h_ref[hel], mat)
    real = (one[:n_b, :n_b] + one[n_b:, n_b:]) - (two[:n_b, :n_b] + two[n_b:, n_b:])
    imag = (one[:n_b, n_b:] - one[n_b:, :n_b]) - (two[:n_b, n_b:] - two[n_b:, :n_b])
    return real, imag


def local_kernel(planes, v_ref, u_ref, phi_ref, out_ref, g_ref, h_ref, sh_ref):
    n_h, _, n_b, _ = out_ref.shape
    width = u_ref.shape[-1]
    kinds = (g_ref, h_ref)

    def block(step, carry):
        row = pl.multiple_of(step * ROWS, ROWS)
        rows = pl.ds(row, ROWS)
        for plane in range(planes):
            dirs = (1, 2, 0) if plane + 1 < planes else (1, 2)
            for part in range(2):
                for col in range(3):
                    start = (col * planes + plane) * width
                    here = pl.ds(pl.multiple_of(part * n_b + row, ROWS), ROWS)
                    field = v_ref[here, pl.ds(start, width)].astype(jnp.float32)
                    sh_ref[0, part, col] = shift_y(field)
                    sh_ref[1, part, col] = shift_z(field)
                    if plane + 1 < planes:
                        sh_ref[2, part, col] = v_ref[here, pl.ds(start + width, width)].astype(jnp.float32)

            def store(kind, hel, part, col, half, value, plane=plane):
                start = (col * planes + plane) * width + half * HALF
                there = pl.ds(pl.multiple_of(part * n_b + row, ROWS), ROWS)
                kinds[kind][hel, there, pl.ds(start, HALF)] = value

            weighted_links(u_ref, phi_ref, sh_ref, dirs, plane, n_h, store)
        return carry

    lax.fori_loop(0, n_b // ROWS, block, 0)

    def multiply(hel, carry):
        real, imag = products(v_ref[...], g_ref, h_ref, hel)
        out_ref[hel, 0] = real
        out_ref[hel, 1] = imag
        return carry

    lax.fori_loop(0, n_h, multiply, 0)


def halo_kernel(planes, v_ref, up_ref, u_ref, phi_ref, part_ref, out_ref, g_ref, h_ref, sh_ref):
    n_h, _, n_b, _ = part_ref.shape
    n_dev = out_ref.shape[0]
    own = n_b // n_dev
    width = u_ref.shape[-1]
    plane = planes - 1
    kinds = (g_ref, h_ref)

    def block(step, carry):
        row = pl.multiple_of(step * ROWS, ROWS)
        rows = pl.ds(row, ROWS)
        for part in range(2):
            for col in range(3):
                sh_ref[0, part, col] = up_ref[part, col, rows, :].astype(jnp.float32)

        def store(kind, hel, part, col, half, value):
            there = pl.ds(pl.multiple_of(part * n_b + row, ROWS), ROWS)
            kinds[kind][hel, there, pl.ds(col * width + half * HALF, HALF)] = value

        weighted_links(u_ref, phi_ref, sh_ref, (0,), plane, n_h, store)
        return carry

    lax.fori_loop(0, n_b // ROWS, block, 0)

    def multiply(hel, carry):
        mat = jnp.concatenate(
            [v_ref[:, pl.ds((col * planes + plane) * width, width)] for col in range(3)], 1
        )
        both = products(mat, g_ref, h_ref, hel)
        for part in range(2):
            total = (both[part] + part_ref[hel, part]).astype(jnp.bfloat16)
            out_ref[:, hel, part] = total.reshape(n_dev, own, n_b)
        return carry

    lax.fori_loop(0, n_h, multiply, 0)


def quark_kernel(got_ref, tau_ref, out_ref, left_ref):
    n_dev, n_h, _, own, n_b = got_ref.shape

    @pl.when(pl.program_id(0) == 0)
    def _():
        row = lax.broadcasted_iota(jnp.int32, (n_b, 2 * n_b), 0)
        col = lax.broadcasted_iota(jnp.int32, (n_b, 2 * n_b), 1)
        even = (col == 2 * row).astype(jnp.bfloat16)
        odd = (col == 2 * row + 1).astype(jnp.bfloat16)
        for hel in range(n_h):
            ops = []
            for part in range(2):
                total = got_ref[0, hel, part].astype(jnp.float32)
                for dev in range(1, n_dev):
                    total = total + got_ref[dev, hel, part].astype(jnp.float32)
                ops.append(total.astype(jnp.bfloat16))
            first = jnp.concatenate(ops, 0)
            second = jnp.concatenate([-ops[1], ops[0]], 0)
            left = jnp.dot(first, even, preferred_element_type=jnp.float32) + jnp.dot(
                second, odd, preferred_element_type=jnp.float32
            )
            left_ref[pl.ds(hel * 2 * own, 2 * own), :] = left.astype(jnp.bfloat16)

    res = jnp.dot(left_ref[...], tau_ref[0], preferred_element_type=jnp.float32)
    for hel in range(n_h):
        for part in range(2):
            start = (hel * 2 + part) * own
            out_ref[hel, 0, part] = res[start : start + own]


def phases(momenta, weights, coord_x, n_x):
    site = jnp.arange(LY * LZ, dtype=jnp.int32)
    yy = site // LZ
    zz = site % LZ
    step = jnp.concatenate([jnp.zeros((1, 3), jnp.int32), jnp.eye(3, dtype=jnp.int32)], 0)
    pos_x = coord_x[None, :, None] + step[:, 0, None, None]
    pos_y = yy[None, None, :] + step[:, 1, None, None]
    pos_z = zz[None, None, :] + step[:, 2, None, None]
    mom = momenta[:, :, None, None, None]
    part_x = (mom[:, 0] * pos_x % n_x).astype(jnp.float32) / n_x
    part_y = (mom[:, 1] * pos_y % LY).astype(jnp.float32) / LY
    part_z = (mom[:, 2] * pos_z % LZ).astype(jnp.float32) / LZ
    theta = 2.0 * math.pi * (part_x + part_y + part_z)
    wave = jnp.stack([jnp.cos(theta), -jnp.sin(theta)], 1)
    wts = weights[:, :, :, None, None, None]
    here = 0.0
    ahead = 0.0
    sign = jnp.array([1.0, -1.0], jnp.float32)[None, None, :, None, None]
    for k in range(momenta.shape[0]):
        here = here + wts[:, k] * wave[k, :, 0][None, None]
        ahead = ahead + wts[:, k] * jnp.swapaxes(wave[k, :, 1:], 0, 1)[None]
    return jnp.stack([here, ahead * sign], 0)


def shards(eigvecs, links, momenta, coef_num, coef_den, peram):
    n_space = lax.axis_size("space")
    n_op = lax.axis_size("op")
    n_tm = lax.axis_size("tm")
    _, _, n_b, _, planes, width = eigvecs.shape
    n_x = planes * n_space
    own = n_b // n_space
    n_h = coef_num.shape[0] // n_op
    my_op = lax.axis_index("op")
    my_space = lax.axis_index("space")

    group = n_space * n_op
    pairs = max(1, SPINS // group)
    depth = min(n_b, n_b * SPINS // group)
    first = (my_space * n_op + my_op) * (pairs * depth)
    piece = lax.dynamic_slice(
        peram.reshape(n_b, SPINS, 2, n_b),
        (first % n_b, first // n_b, 0, 0),
        (depth, pairs, 2, n_b),
    )
    piece = jnp.swapaxes(piece, 0, 1).reshape(pairs * depth * 2, n_b)
    piece = from_behind(piece, "tm", n_tm - 1)
    tau = lax.all_gather(piece, ("space", "op"), axis=0, tiled=True).reshape(SPINS, 2 * n_b, n_b)

    upper = jnp.transpose(eigvecs[0, :, :, :, 0, :], (0, 2, 1, 3))
    upper = from_behind(upper, "space", -1)

    small = jnp.concatenate([momenta.reshape(-1), coef_num.reshape(-1)])
    parts = [small] + [from_behind(small, "op", shift) for shift in range(1, n_op)]
    n_mom = momenta.shape[0]
    moms = jnp.concatenate([part[: n_mom * 3].reshape(n_mom, 3) for part in parts], 0)
    nums = jnp.concatenate(
        [part[n_mom * 3 :].reshape(coef_num.shape) for part in parts], 1
    )
    weights = nums.astype(jnp.float32) / coef_den.astype(jnp.float32)[:, None, None]
    scale = 1.0 / math.sqrt(3.0 * n_x * LY * LZ)
    weights = lax.dynamic_slice_in_dim(weights, my_op * n_h, n_h, 0) * scale
    coord_x = planes * my_space + jnp.arange(planes, dtype=jnp.int32)
    phi = phases(moms, weights, coord_x, n_x)

    mat = eigvecs.reshape(2 * n_b, 3 * planes * width)
    link = links[0]
    params = pltpu.CompilerParams(vmem_limit_bytes=48 * 2**20)
    depth_k = 3 * planes * width
    partial = pl.pallas_call(
        functools.partial(local_kernel, planes),
        out_shape=jax.ShapeDtypeStruct((n_h, 2, n_b, n_b), jnp.float32),
        scratch_shapes=[
            pltpu.VMEM((n_h, 2 * n_b, depth_k), jnp.bfloat16),
            pltpu.VMEM((n_h, 2 * n_b, depth_k), jnp.bfloat16),
            pltpu.VMEM((3, 2, 3, ROWS, width), jnp.float32),
        ],
        compiler_params=params,
        cost_estimate=pl.CostEstimate(
            flops=16 * n_h * n_b * n_b * depth_k, bytes_accessed=2**22, transcendentals=0
        ),
        name="local_sites",
    )(mat, link, phi)
    sums = pl.pallas_call(
        functools.partial(halo_kernel, planes),
        out_shape=jax.ShapeDtypeStruct((n_space, n_h, 2, own, n_b), jnp.bfloat16),
        scratch_shapes=[
            pltpu.VMEM((n_h, 2 * n_b, 3 * width), jnp.bfloat16),
            pltpu.VMEM((n_h, 2 * n_b, 3 * width), jnp.bfloat16),
            pltpu.VMEM((1, 2, 3, ROWS, width), jnp.float32),
        ],
        compiler_params=params,
        cost_estimate=pl.CostEstimate(
            flops=16 * n_h * n_b * n_b * 3 * width, bytes_accessed=2**22, transcendentals=0
        ),
        name="halo_plane",
    )(mat, upper, link, phi, partial)
    got = lax.all_to_all(sums, "space", 0, 0, tiled=True)

    lines = pl.pallas_call(
        quark_kernel,
        grid=(SPINS,),
        in_specs=[
            pl.BlockSpec((n_space, n_h, 2, own, n_b), lambda s: (0, 0, 0, 0, 0)),
            pl.BlockSpec((1, 2 * n_b, n_b), lambda s: (s, 0, 0)),
        ],
        out_specs=pl.BlockSpec((n_h, 1, 2, own, n_b), lambda s: (0, s, 0, 0, 0)),
        out_shape=jax.ShapeDtypeStruct((n_h, SPINS, 2, own, n_b), jnp.float32),
        scratch_shapes=[pltpu.VMEM((n_h * 2 * own, 2 * n_b), jnp.bfloat16)],
        compiler_params=params,
        cost_estimate=pl.CostEstimate(
            flops=2 * SPINS * n_h * 2 * own * 2 * n_b * n_b, bytes_accessed=7 * 2**20, transcendentals=0
        ),
        name="quark_products",
    )(got, tau)
    return lines.reshape(1, n_h, 4, 4, 2, own, n_b)


def solution(mesh):
    return jax.shard_map(
        shards,
        mesh=mesh,
        in_specs=(
            P("tm", None, None, None, "space", None),
            P("tm", None, None, None, None, "space", None),
            P("op", None),
            P(None, "op", None),
            P(),
            P("tm", None, None, None, None, None),
        ),
        out_specs=P("tm", "op", None, None, None, "space", None),
        check_vma=False,
    )
```

profile of v0, /device:TPU:1, one launch (start us, length us, event | category | flops | bytes accessed | tf_op | source)
XLA Modules:
  0.0 96.8 jit_solution(5201174541956133387)
XLA Ops:
  6.6 1.2 %constant_dynamic-slice_fusion = bf16[256,1,2,256]{3,2,1,0:T(2,128)(2,1)S(1)} fusion(bf16[256,16,2,256]{3,2,1,0:T(2,128)(2,1)} %bitcast.54, s32[]{:T(128)S(6)} %select_n.73), kind=kLoop, calls=%fused_computation.62 | loop fusion | bytes 524292 | tf_op jit(solution)/shard_map/dynamic_slice | solution.py:230
  7.8 0.1 reshape_transpose.3
  7.9 3.2 %collective-permute-start.2 = (bf16[512,256]{1,0:T(8,128)(2,1)S(1)}, bf16[512,256]{1,0:T(8,128)(2,1)S(1)}, u32[]{:S(2)}, u32[]{:S(2)}) collective-permute-start(bf16[512,256]{1,0:T(8,128)(2,1)S(1)} %reshape_transpose.3), channel_id=1, source_target_pairs={{0,2},{2,0},{1,3},{3,1},{4,6},{6,4},{5,7},{7,5},{8,10},{10,8},{9,1... | collective-permute-start | bytes 786440 | tf_op jit(solution)/shard_map/ppermute | solution.py:22
  11.1 11.6 %collective-permute-done.2 = bf16[512,256]{1,0:T(8,128)(2,1)S(1)} collective-permute-done((bf16[512,256]{1,0:T(8,128)(2,1)S(1)}, bf16[512,256]{1,0:T(8,128)(2,1)S(1)}, u32[]{:S(2)}, u32[]{:S(2)}) %collective-permute-start.2) | collective-permute-done | bytes 262176 | tf_op jit(solution)/shard_map/ppermute | solution.py:22
  22.7 0.7 copy-done.2
  23.5 0.8 copy.18
  24.2 0.1 reshape.352
  24.3 0.8 reshape.351
  25.1 0.1 pad_add_fusion
  25.2 1.2 %collective-permute-start.1 = (s32[30]{0:T(128)S(1)}, s32[30]{0:T(128)S(1)}, u32[]{:S(2)}, u32[]{:S(2)}) collective-permute-start(s32[30]{0:T(128)S(1)} %pad_add_fusion), channel_id=1, source_target_pairs={{0,1},{1,0},{2,3},{3,2},{4,5},{5,4},{6,7},{7,6},{8,9},{9,8},{10,11... | collective-permute-start | bytes 368 | tf_op jit(solution)/shard_map/ppermute | solution.py:22
  26.4 1.5 %copy.26 = bf16[1,2,256,3,1,256]{5,2,3,1,4,0:T(8,128)(2,1)S(1)} copy(bf16[1,2,256,3,1,256]{5,4,3,2,1,0:T(2,128)(2,1)} %bitcast.51) | data formatting | bytes 1572864
  27.9 0.8 collective-permute-start
  28.7 3.9 %reshape.350.v_ref = bf16[512,1536]{1,0:T(8,128)(2,1)S(1)} reshape(bf16[1,2,256,3,2,256]{5,4,3,2,1,0:T(2,128)(2,1)} %param.7) | data formatting | bytes 3145728 | tf_op jit(solution)/shard_map/reshape | solution.py:255
  33.0 0.1 reshape.354
  33.1 0.1 reshape.353
  33.3 0.1 copy.19
  33.4 0.2 slice_reduce_fusion.2
  33.6 0.1 fusion.9
  33.8 0.1 fusion.2
  33.9 0.1 fusion.4
  34.0 0.5 fusion
  34.5 0.1 copy.21
  34.6 0.1 copy.22
  34.7 0.1 copy.23
  34.8 0.1 copy.20
  35.0 0.1 multiply_add_fusion
  35.1 13.7 %local_sites.1.part_ref = f32[2,2,256,256]{3,2,1,0:T(8,128)S(1)} custom-call(bf16[512,1536]{1,0:T(8,128)(2,1)S(1)} %reshape.350.v_ref, f32[3,3,3,2,2,256]{5,4,3,2,1,0:T(2,128)S(1)} %bitcast.49, f32[2,2,3,2,2,256]{5,4,3,2,1,0:T(2,128)S(1)} %pad_maximum_fusion.phi_ref), custom_call_target="tpu_custom_call" | custom-call | flops 3221225472 | bytes 4194304 | tf_op jit(solution)/shard_map/local_sites/pallas_call | solution.py:259
  48.8 3.7 %halo_plane.1 = bf16[8,2,2,32,256]{4,3,2,1,0:T(8,128)(2,1)S(1)} custom-call(bf16[512,1536]{1,0:T(8,128)(2,1)S(1)} %reshape.350.v_ref, bf16[2,3,256,256]{3,2,1,0:T(8,128)(2,1)S(1)} %collective-permute-done.up_ref, f32[3,3,3,2,2,256]{5,4,3,2,1,0:T(2,128)S(1)} %bitcast.50, f32[2,2,3,2,2,256]{5,4,3,2,1,0:T(2,128)S(1)} %pad_maximum_fusion.phi_ref, ...), custom_call_target="tpu_custom_call" | custom-call | flops 1610612736 | bytes 4194304 | tf_op jit(solution)/shard_map/halo_plane/pallas_call | solution.py:273
  52.6 14.1 %all_to_all.5.got_ref = bf16[8,2,2,32,256]{4,3,2,1,0:T(8,128)(2,1)S(1)} all-to-all(bf16[8,2,2,32,256]{4,3,2,1,0:T(8,128)(2,1)S(1)} %halo_plane.1), channel_id=1, replica_groups=mesh['space'=8,'tm'=2,'op'=2] {'space'}, dimensions={0} | all-to-all | bytes 1048576 | tf_op jit(solution)/shard_map/all_to_all | solution.py:287
  66.7 13.7 %all-gather.2.cloned.1.call-done = bf16[8192,256]{1,0:T(8,128)(2,1)} async-done(((bf16[512,256]{1,0:T(8,128)(2,1)}), bf16[8192,256]{1,0:T(8,128)(2,1)}) %all-gather.2.cloned.1.call-update) | async-done | bytes 4194320 | tf_op jit(solution)/shard_map/all_gather | solution.py:237
  80.4 2.2 %copy-done = bf16[8192,256]{1,0:T(8,128)(2,1)S(1)} copy-done((bf16[8192,256]{1,0:T(8,128)(2,1)S(1)}, bf16[8192,256]{1,0:T(8,128)(2,1)}, u32[]{:S(2)}) %copy-start) | copy-done | bytes 4194328
  82.6 7.4 %quark_products.1 = f32[2,16,2,32,256]{4,3,2,1,0:T(8,128)} custom-call(bf16[8,2,2,32,256]{4,3,2,1,0:T(8,128)(2,1)S(1)} %all_to_all.5.got_ref, bf16[16,512,256]{2,1,0:T(8,128)(2,1)S(1)} %bitcast.48), custom_call_target="tpu_custom_call" | custom-call | flops 536870912 | bytes 7340032 | tf_op jit(solution)/shard_map/quark_products/pallas_call | solution.py:289
  (31 shorter events, 0.7 us)
Async XLA Ops:
  6.5 28.4 %copy-start.4 = (f32[2]{0:T(128)S(1)}, f32[2]{0:T(128)}, u32[]{:S(2)}) copy-start(f32[2]{0:T(128)} %constant.116.clone) | copy-start | bytes 28
  6.5 26.9 %copy-start.3 = (s32[2,3]{1,0:T(2,128)S(1)}, s32[2,3]{1,0:T(2,128)}, u32[]{:S(2)}) copy-start(s32[2,3]{1,0:T(2,128)} %param.9) | copy-start | bytes 76
  6.5 26.1 %copy-start.5 = (s32[4]{0:T(128)S(1)}, s32[4]{0:T(128)}, u32[]{:S(2)}) copy-start(s32[4]{0:T(128)} %param.11) | copy-start | bytes 52
  6.5 28.6 %copy-start.1 = (f32[1,3,3,3,2,2,256]{6,5,4,3,2,1,0:T(2,128)S(1)}, f32[1,3,3,3,2,2,256]{6,5,4,3,2,1,0:T(2,128)}, u32[]{:S(2)}) copy-start(f32[1,3,3,3,2,2,256]{6,5,4,3,2,1,0:T(2,128)} %param.8) | copy-start | bytes 331780
  6.5 73.8 %all-gather.2.cloned.1.call-start = ((), (), s32[]{:S(2)}) async-start(), calls=%async_computation.1 | async-start | bytes 4456448 | tf_op jit(solution)/shard_map/all_gather | solution.py:237
  7.9 14.9 %collective-permute-start.2 = (bf16[512,256]{1,0:T(8,128)(2,1)S(1)}, bf16[512,256]{1,0:T(8,128)(2,1)S(1)}, u32[]{:S(2)}, u32[]{:S(2)}) collective-permute-start(bf16[512,256]{1,0:T(8,128)(2,1)S(1)} %reshape_transpose.3), channel_id=1, source_target_pairs={{0,2},{2,0},{1,3},{3,1},{4,6},{6,4},{5,7},{7,5},{8,10},{10,8},{9,1... | collective-permute-start | bytes 786440 | tf_op jit(solution)/shard_map/ppermute | solution.py:22
  22.7 0.7 copy-start.2
  25.2 7.8 %collective-permute-start.1 = (s32[30]{0:T(128)S(1)}, s32[30]{0:T(128)S(1)}, u32[]{:S(2)}, u32[]{:S(2)}) collective-permute-start(s32[30]{0:T(128)S(1)} %pad_add_fusion), channel_id=1, source_target_pairs={{0,1},{1,0},{2,3},{3,2},{4,5},{5,4},{6,7},{7,6},{8,9},{9,8},{10,11... | collective-permute-start | bytes 368 | tf_op jit(solution)/shard_map/ppermute | solution.py:22
  27.9 20.9 %collective-permute-start = (bf16[2,3,256,256]{3,2,1,0:T(8,128)(2,1)S(1)}, bf16[2,3,256,256]{3,2,1,0:T(8,128)(2,1)S(1)}, u32[]{:S(2)}, u32[]{:S(2)}) collective-permute-start(bf16[2,3,256,256]{3,2,1,0:T(8,128)(2,1)S(1)} %bitcast.52), channel_id=1, source_target_pairs={{0,28},{4,0},{8,4},{12,8},{16,12},{20,16},{24,20},{28,24},{1,29},{... | collective-permute-start | bytes 2359304 | tf_op jit(solution)/shard_map/ppermute | solution.py:22
  80.4 2.2 %copy-start = (bf16[8192,256]{1,0:T(8,128)(2,1)S(1)}, bf16[8192,256]{1,0:T(8,128)(2,1)}, u32[]{:S(2)}) copy-start(bf16[8192,256]{1,0:T(8,128)(2,1)} %all-gather.2.cloned.1.call-done) | copy-start | bytes 12582916
Sparse Core Ops, SparseCore 0:
  23.6 56.7 all-gather.1
where the time goes:
time: 97.1 us; the launch traced here: 96.8 us
  waiting for transfers between devices  25.4 us (26%)
  Pallas kernels  24.8 us (26%)
  blocking collectives  14.1 us (15%)
  between operations  13.6 us (14%)
  local copies, waits for them, and re-layouts  12.3 us (13%)
  starting transfers between devices  5.24 us (5%)
  other arithmetic  1.39 us (1%)
    all_to_all x1, blocking collectives, shards(): got = lax.all_to_all(sums, 'space', 0, 0, tiled=True)  14.1 us
    all_gather x1, waiting for transfers between devices, shards(): lax.all_gather(piece, ('space', 'op'), axis=0, tiled=True)  13.7 us
    pallas_call x1, Pallas kernels, shards(): pl.pallas_call(functools.partial(local_kernel, planes), out_shape=jax.Sha...  13.7 us
    ppermute x3, waiting for transfers between devices, from_behind(): return lax.ppermute(value, axis, pairs)  11.7 us
    pallas_call x1, Pallas kernels, shards(): pl.pallas_call(quark_kernel, grid=(SPINS,), in_specs=[pl.BlockSpec((n_spa...  7.36 us
    unnamed x14, local copies, waits for them, and re-layouts  5.22 us
    ppermute x3, starting transfers between devices, from_behind(): return lax.ppermute(value, axis, pairs)  5.21 us
    reshape x1, local copies, waits for them, and re-layouts, shards(): mat = eigvecs.reshape(2 * n_b, 3 * planes * width)  3.88 us
  transfers between devices with their start and end apart: 4, of which 2 were waited for; matrix products, arithmetic and copies ran while one was open for 10% of the time, Pallas kernels for 18%

commit v1 on v0

v1 whole, which is shorter than its diff:
```python
import functools
import math

import jax
import jax.numpy as jnp
from jax import lax
from jax.experimental import pallas as pl
from jax.experimental.pallas import tpu as pltpu
from jax.sharding import PartitionSpec as P

LY = 32
LZ = 8
NDIR = 3
SPINS = 16
ROWS = 16
HALF = 128


def from_behind(value, axis, steps):
    count = lax.axis_size(axis)
    pairs = [(source, (source + steps) % count) for source in range(count)]
    return lax.ppermute(value, axis, pairs)


def across(value, axis, mask):
    pairs = [(source, source ^ mask) for source in range(lax.axis_size(axis))]
    return lax.ppermute(value, axis, pairs)


def dot_nt(left, right):
    return lax.dot_general(
        left, right, (((1,), (1,)), ((), ())), preferred_element_type=jnp.float32
    )


def shift_y(arr):
    return pltpu.roll(arr, arr.shape[1] - LZ, 1)


def shift_z(arr):
    width = arr.shape[1]
    lane = lax.broadcasted_iota(jnp.int32, arr.shape, 1)
    near = pltpu.roll(arr, width - 1, 1)
    far = pltpu.roll(arr, LZ - 1, 1)
    return jnp.where((lane & (LZ - 1)) == LZ - 1, far, near)


def weighted_links(u_ref, phi_ref, shifted, dirs, plane, n_h, store):
    width = u_ref.shape[-1]
    for half in range(width // HALF):
        lanes = pl.ds(half * HALF, HALF)
        for col in range(3):
            acc = {}
            for slot, direc in enumerate(dirs):
                f_r = None
                f_i = None
                for col_two in range(3):
                    u_r = u_ref[direc, col, col_two, 0, pl.ds(plane, 1), lanes]
                    u_i = u_ref[direc, col, col_two, 1, pl.ds(plane, 1), lanes]
                    v_r = shifted[slot, 0, col_two, :, lanes]
                    v_i = shifted[slot, 1, col_two, :, lanes]
                    term_r = u_r * v_r - u_i * v_i
                    term_i = u_r * v_i + u_i * v_r
                    f_r = term_r if f_r is None else f_r + term_r
                    f_i = term_i if f_i is None else f_i + term_i
                for kind in range(2):
                    for hel in range(n_h):
                        p_r = phi_ref[kind, hel, direc, 0, pl.ds(plane, 1), lanes]
                        p_i = phi_ref[kind, hel, direc, 1, pl.ds(plane, 1), lanes]
                        g_r = p_r * f_r - p_i * f_i
                        g_i = p_r * f_i + p_i * f_r
                        if (kind, hel) in acc:
                            old_r, old_i = acc[kind, hel]
                            g_r, g_i = old_r + g_r, old_i + g_i
                        acc[kind, hel] = (g_r, g_i)
            for (kind, hel), both in acc.items():
                for part in range(2):
                    store(kind, hel, part, col, half, both[part].astype(jnp.bfloat16))


def products(mat, g_ref, h_ref, hel):
    n_b = mat.shape[0] // 2
    one = dot_nt(mat, g_ref[hel])
    two = dot_nt(h_ref[hel], mat)
    real = (one[:n_b, :n_b] + one[n_b:, n_b:]) - (two[:n_b, :n_b] + two[n_b:, n_b:])
    imag = (one[:n_b, n_b:] - one[n_b:, :n_b]) - (two[:n_b, n_b:] - two[n_b:, :n_b])
    return real, imag


def plane_kernel(plane, dirs, has_part, n_out, *refs):
    refs = list(refs)
    v_ref = refs.pop(0)
    next_ref = refs.pop(0) if 0 in dirs else None
    u_ref, phi_ref = refs.pop(0), refs.pop(0)
    part_ref = refs.pop(0) if has_part else None
    where_ref = refs.pop(0) if n_out else None
    out_refs = [refs.pop(0) for _ in range(n_out or 1)]
    g_ref, h_ref, sh_ref = refs[:3]
    n_h = phi_ref.shape[1]
    _, _, n_b, width = v_ref.shape
    kinds = (g_ref, h_ref)

    def block(step, carry):
        row = pl.multiple_of(step * ROWS, ROWS)
        rows = pl.ds(row, ROWS)
        for slot, direc in enumerate(dirs):
            for part in range(2):
                for col in range(3):
                    if direc == 0:
                        sh_ref[slot, part, col] = next_ref[part, col, rows, :].astype(jnp.float32)
                    else:
                        field = v_ref[part, col, rows, :].astype(jnp.float32)
                        sh_ref[slot, part, col] = shift_y(field) if direc == 1 else shift_z(field)

        def store(kind, hel, part, col, half, value):
            there = pl.ds(pl.multiple_of(part * n_b + row, ROWS), ROWS)
            kinds[kind][hel, there, pl.ds(col * width + half * HALF, HALF)] = value

        weighted_links(u_ref, phi_ref, sh_ref, dirs, plane, n_h, store)
        return carry

    lax.fori_loop(0, n_b // ROWS, block, 0)

    def multiply(hel, carry):
        mat = jnp.concatenate([v_ref[:, col].reshape(2 * n_b, width) for col in range(3)], 1)
        both = products(mat, g_ref, h_ref, hel)
        for part in range(2):
            total = both[part] + part_ref[hel, part] if has_part else both[part]
            if n_out:
                refs[3][hel * 2 + part] = total
            else:
                out_refs[0][hel, part] = total
        return carry

    lax.fori_loop(0, n_h, multiply, 0)
    if n_out:
        own = n_b // n_out
        for mask in range(n_out):
            rows = pl.ds(pl.multiple_of((where_ref[0] ^ mask) * own, own), own)
            pieces = [refs[3][which, rows, :] for which in range(2 * n_h)]
            out_refs[mask][...] = jnp.concatenate(pieces, 0).astype(jnp.bfloat16)


def plane_call(plane, dirs, vec, ahead, link, phi, part=None, where=None, n_out=0):
    n_h = phi.shape[1]
    _, _, n_b, width = vec.shape
    vmem = pl.BlockSpec(memory_space=pltpu.VMEM)
    args = [vec] + ([ahead] if 0 in dirs else []) + [link, phi]
    args += [part] if part is not None else []
    specs = [vmem] * len(args)
    scratch = [
        pltpu.VMEM((n_h, 2 * n_b, 3 * width), jnp.bfloat16),
        pltpu.VMEM((n_h, 2 * n_b, 3 * width), jnp.bfloat16),
        pltpu.VMEM((len(dirs), 2, 3, ROWS, width), jnp.float32),
    ]
    if n_out:
        args.append(where)
        specs.append(pl.BlockSpec(memory_space=pltpu.SMEM))
        scratch.append(pltpu.VMEM((2 * n_h, n_b, n_b), jnp.float32))
        shape = jax.ShapeDtypeStruct((2 * n_h * (n_b // n_out), n_b), jnp.bfloat16)
        out_shape = [shape] * n_out
        out_specs = [vmem] * n_out
    else:
        out_shape = jax.ShapeDtypeStruct((n_h, 2, n_b, n_b), jnp.float32)
        out_specs = vmem
    return pl.pallas_call(
        functools.partial(plane_kernel, plane, dirs, part is not None, n_out),
        in_specs=specs,
        out_specs=out_specs,
        out_shape=out_shape,
        scratch_shapes=scratch,
        compiler_params=pltpu.CompilerParams(vmem_limit_bytes=40 * 2**20),
        cost_estimate=pl.CostEstimate(
            flops=(16 + 8 * len(dirs)) * n_h * n_b * n_b * 3 * width,
            bytes_accessed=2**22,
            transcendentals=0,
        ),
        name="plane%d_%s" % (plane, "".join(str(direc) for direc in dirs)),
    )(*args)


def quark_kernel(n_got, n_tau, where_ref, *refs):
    got_refs = refs[:n_got]
    tau_refs = refs[n_got : n_got + n_tau]
    out_ref, left_ref = refs[n_got + n_tau :]
    n_h, n_pair, _, own, n_b = out_ref.shape
    row = lax.broadcasted_iota(jnp.int32, (n_b, 2 * n_b), 0)
    col = lax.broadcasted_iota(jnp.int32, (n_b, 2 * n_b), 1)
    even = (col == 2 * row).astype(jnp.bfloat16)
    odd = (col == 2 * row + 1).astype(jnp.bfloat16)
    total = got_refs[0][...].astype(jnp.float32)
    for ref in got_refs[1:]:
        total = total + ref[...].astype(jnp.float32)
    swap = []
    for hel in range(n_h):
        start = hel * 2 * own
        swap += [-total[start + own : start + 2 * own], total[start : start + own]]
    left = jnp.dot(total.astype(jnp.bfloat16), even, preferred_element_type=jnp.float32)
    left += jnp.dot(
        jnp.concatenate(swap, 0).astype(jnp.bfloat16), odd, preferred_element_type=jnp.float32
    )
    left_ref[...] = left.astype(jnp.bfloat16)
    depth = tau_refs[0].shape[0]
    whole = depth == 2 * n_b
    if not whole:
        out_ref[...] = jnp.zeros_like(out_ref)
    for which in range(n_tau):
        first = where_ref[which] * depth
        pair = first // (2 * n_b)
        if whole:
            lhs = left_ref[...]
        else:
            lhs = left_ref[:, pl.ds(pl.multiple_of(first - pair * 2 * n_b, depth), depth)]
        res = jnp.dot(lhs, tau_refs[which][...], preferred_element_type=jnp.float32)
        for hel in range(n_h):
            for part in range(2):
                start = (hel * 2 + part) * own
                if whole:
                    out_ref[hel, pair, part] = res[start : start + own]
                else:
                    out_ref[hel, pair, part] += res[start : start + own]


def phases(momenta, weights, coord_x, n_x):
    site = jnp.arange(LY * LZ, dtype=jnp.int32)
    yy = site // LZ
    zz = site % LZ
    step = jnp.concatenate([jnp.zeros((1, 3), jnp.int32), jnp.eye(3, dtype=jnp.int32)], 0)
    pos_x = coord_x[None, :, None] + step[:, 0, None, None]
    pos_y = yy[None, None, :] + step[:, 1, None, None]
    pos_z = zz[None, None, :] + step[:, 2, None, None]
    mom = momenta[:, :, None, None, None]
    part_x = (mom[:, 0] * pos_x % n_x).astype(jnp.float32) / n_x
    part_y = (mom[:, 1] * pos_y % LY).astype(jnp.float32) / LY
    part_z = (mom[:, 2] * pos_z % LZ).astype(jnp.float32) / LZ
    theta = 2.0 * math.pi * (part_x + part_y + part_z)
    wave = jnp.stack([jnp.cos(theta), -jnp.sin(theta)], 1)
    wts = weights[:, :, :, None, None, None]
    here = 0.0
    ahead = 0.0
    sign = jnp.array([1.0, -1.0], jnp.float32)[None, None, :, None, None]
    for k in range(momenta.shape[0]):
        here = here + wts[:, k] * wave[k, :, 0][None, None]
        ahead = ahead + wts[:, k] * jnp.swapaxes(wave[k, :, 1:], 0, 1)[None]
    return jnp.stack([here, ahead * sign], 0)


def shards(eigvecs, links, momenta, coef_num, coef_den, peram):
    n_space = lax.axis_size("space")
    n_op = lax.axis_size("op")
    n_tm = lax.axis_size("tm")
    _, _, n_b, _, planes, width = eigvecs.shape
    n_x = planes * n_space
    own = n_b // n_space
    n_h = coef_num.shape[0] // n_op
    my_op = lax.axis_index("op")
    my_space = lax.axis_index("space")

    group = n_space * n_op
    depth = n_b * SPINS // group
    first = (my_space * n_op + my_op) * depth
    piece = lax.dynamic_slice(
        peram.reshape(n_b, SPINS, 2, n_b), (first % n_b, first // n_b, 0, 0), (depth, 1, 2, n_b)
    ).reshape(depth * 2, n_b)
    piece = from_behind(piece, "tm", n_tm - 1)

    vecs = [jnp.transpose(eigvecs[0, :, :, :, plane, :], (0, 2, 1, 3)) for plane in range(planes)]
    upper = from_behind(vecs[0], "space", -1)

    held = [(piece, my_space, my_op)]
    for mask in range(2, n_space, 2):
        held.append((across(piece, "space", mask), my_space ^ mask, my_op))
    for mask in range(1, n_op):
        held += [(across(arr, "op", mask), place, oper ^ mask) for arr, place, oper in held[: n_space // 2]]
    held += [(across(arr, "space", 1), place ^ 1, oper) for arr, place, oper in held]
    tau = [arr for arr, _, _ in held]
    tau_place = jnp.stack([place * n_op + oper for _, place, oper in held]).astype(jnp.int32)

    small = jnp.concatenate([momenta.reshape(-1), coef_num.reshape(-1)])
    parts = [small] + [from_behind(small, "op", shift) for shift in range(1, n_op)]
    n_mom = momenta.shape[0]
    moms = jnp.concatenate([part[: n_mom * 3].reshape(n_mom, 3) for part in parts], 0)
    nums = jnp.concatenate(
        [part[n_mom * 3 :].reshape(coef_num.shape) for part in parts], 1
    )
    weights = nums.astype(jnp.float32) / coef_den.astype(jnp.float32)[:, None, None]
    scale = 1.0 / math.sqrt(3.0 * n_x * LY * LZ)
    weights = lax.dynamic_slice_in_dim(weights, my_op * n_h, n_h, 0) * scale
    coord_x = planes * my_space + jnp.arange(planes, dtype=jnp.int32)
    phi = phases(moms, weights, coord_x, n_x)

    link = links[0]
    last = planes - 1
    partial = plane_call(last, (1, 2), vecs[last], None, link, phi)
    for plane in range(last):
        partial = plane_call(plane, (1, 2, 0), vecs[plane], vecs[plane + 1], link, phi, partial)
    where = my_space.astype(jnp.int32).reshape(1)
    sums = plane_call(last, (0,), vecs[last], upper, link, phi, partial, where, n_space)
    got = [sums[0]] + [across(sums[mask], "space", mask) for mask in range(1, n_space)]

    vmem = pl.BlockSpec(memory_space=pltpu.VMEM)
    lines = pl.pallas_call(
        functools.partial(quark_kernel, len(got), len(tau)),
        in_specs=[pl.BlockSpec(memory_space=pltpu.SMEM)] + [vmem] * (len(got) + len(tau)),
        out_specs=vmem,
        out_shape=jax.ShapeDtypeStruct((n_h, SPINS, 2, own, n_b), jnp.float32),
        scratch_shapes=[pltpu.VMEM((n_h * 2 * own, 2 * n_b), jnp.bfloat16)],
        compiler_params=pltpu.CompilerParams(vmem_limit_bytes=40 * 2**20),
        cost_estimate=pl.CostEstimate(
            flops=2 * SPINS * n_h * 2 * own * 2 * n_b * n_b, bytes_accessed=7 * 2**20, transcendentals=0
        ),
        name="quark_products",
    )(tau_place, *got, *tau)
    return lines.reshape(1, n_h, 4, 4, 2, own, n_b)


def solution(mesh):
    return jax.shard_map(
        shards,
        mesh=mesh,
        in_specs=(
            P("tm", None, None, None, "space", None),
            P("tm", None, None, None, None, "space", None),
            P("op", None),
            P(None, "op", None),
            P(),
            P("tm", None, None, None, None, None),
        ),
        out_specs=P("tm", "op", None, None, None, "space", None),
        check_vma=False,
    )
```

time: 97.1 us -> 94.5 us (0.973)
  the two profiles are of different devices: /device:TPU:1 before, /device:TPU:0 now
where the time goes in v1:
time: 94.5 us; the launch traced here: 94.1 us
  waiting for transfers between devices  30.1 us (32%)
  starting transfers between devices  24.2 us (26%)
  Pallas kernels  23.8 us (25%)
  local copies, waits for them, and re-layouts  14.4 us (15%)
  other arithmetic  1.38 us (1%)
    ppermute x22, waiting for transfers between devices, across(): return lax.ppermute(value, axis, pairs)  21.5 us
    pallas_call x3, Pallas kernels, plane_call(): pl.pallas_call(functools.partial(plane_kernel, plane, dirs, part is not N...  20.5 us
    ppermute x22, starting transfers between devices, across(): return lax.ppermute(value, axis, pairs)  16.9 us
    ppermute x3, waiting for transfers between devices, from_behind(): return lax.ppermute(value, axis, pairs)  8.63 us
    ppermute x3, starting transfers between devices, from_behind(): return lax.ppermute(value, axis, pairs)  7.27 us
    unnamed x26, local copies, waits for them, and re-layouts  7.14 us
    slice x1, local copies, waits for them, and re-layouts, shards(): eigvecs[0, :, :, :, plane, :]  4.4 us
    pallas_call x1, Pallas kernels, shards(): pl.pallas_call(functools.partial(quark_kernel, len(got), len(tau)), in_sp...  3.34 us
  transfers between devices with their start and end apart: 25, of which 9 were waited for; matrix products, arithmetic and copies ran while one was open for 10% of the time, Pallas kernels for 22%

profile of v1, /device:TPU:0, one launch (start us, length us, event | category | flops | bytes accessed | tf_op | source)
XLA Modules:
  0.0 94.1 jit_solution(2941784050523318354)
XLA Ops:
  0.0 0.8 copy.21
  0.9 0.8 reshape.350
  1.7 3.0 %collective-permute-start.1 = (s32[30]{0:T(128)S(1)}, s32[30]{0:T(128)S(1)}, u32[]{:S(2)}, u32[]{:S(2)}) collective-permute-start(s32[30]{0:T(128)S(1)} %pad_add_fusion), channel_id=1, source_target_pairs={{0,1},{1,0},{2,3},{3,2},{4,5},{5,4},{6,7},{7,6},{8,9},{9,8},{10,11... | collective-permute-start | bytes 368 | tf_op jit(solution)/shard_map/ppermute | solution.py:22
  4.7 4.4 %fusion.17 = (bf16[1,2,256,3,1,256]{5,4,3,2,1,0:T(2,128)(2,1)S(1)}, bf16[1,2,256,3,1,256]{5,4,3,2,1,0:T(2,128)(2,1)S(1)}) fusion(bf16[1,2,256,3,2,256]{5,4,3,2,1,0:T(2,128)(2,1)} %param.7), kind=kLoop, calls=%fused_computation.69 | loop fusion | bytes 3145728 | tf_op jit(solution)/shard_map/slice | solution.py:267
  9.3 1.7 %collective-permute-start = (bf16[2,3,256,256]{3,2,1,0:T(8,128)(2,1)S(1)}, bf16[2,3,256,256]{3,2,1,0:T(8,128)(2,1)}, u32[]{:S(2)}, u32[]{:S(2)}) collective-permute-start(bf16[2,3,256,256]{3,2,1,0:T(8,128)(2,1)S(1)} %bitcast.72), channel_id=1, source_target_pairs={{0,28},{4,0},{8,4},{12,8},{16,12},{20,16},{24,20},{28,24},{1,29},{... | collective-permute-start | bytes 2359304 | tf_op jit(solution)/shard_map/ppermute | solution.py:22
  11.0 1.1 %dynamic-slice_bitcast_fusion = bf16[256,1,2,256]{3,2,0,1:T(2,128)(2,1)S(1)} fusion(bf16[256,16,2,256]{3,2,1,0:T(2,128)(2,1)} %bitcast.81, s32[]{:T(128)S(6)} %select_n.73), kind=kLoop, calls=%fused_computation.2 | loop fusion | bytes 524292
  12.1 0.8 reshape.356
  12.9 2.6 %collective-permute-start.9 = (bf16[512,256]{1,0:T(8,128)(2,1)}, bf16[512,256]{1,0:T(8,128)(2,1)S(1)}, u32[]{:S(2)}, u32[]{:S(2)}) collective-permute-start(bf16[512,256]{1,0:T(8,128)(2,1)} %reshape.356), channel_id=1, source_target_pairs={{0,2},{2,0},{1,3},{3,1},{4,6},{6,4},{5,7},{7,5},{8,10},{10,8},{9,1... | collective-permute-start | bytes 786440 | tf_op jit(solution)/shard_map/ppermute | solution.py:22
  18.0 8.6 %collective-permute-done.9.refs_8_ = bf16[512,256]{1,0:T(8,128)(2,1)S(1)} collective-permute-done((bf16[512,256]{1,0:T(8,128)(2,1)}, bf16[512,256]{1,0:T(8,128)(2,1)S(1)}, u32[]{:S(2)}, u32[]{:S(2)}) %collective-permute-start.9) | collective-permute-done | bytes 262176 | tf_op jit(solution)/shard_map/ppermute | solution.py:22
  26.6 1.5 %collective-permute-start.10 = (bf16[512,256]{1,0:T(8,128)(2,1)S(1)}, bf16[512,256]{1,0:T(8,128)(2,1)S(1)}, u32[]{:S(2)}, u32[]{:S(2)}) collective-permute-start(bf16[512,256]{1,0:T(8,128)(2,1)S(1)} %collective-permute-done.9.refs_8_), channel_id=1, source_target_pairs={{0,8},{4,12},{8,0},{12,4},{16,24},{20,28},{24,16},{28,20},{1,9},{5... | collective-permute-start | bytes 786440 | tf_op jit(solution)/shard_map/ppermute | solution.py:27
  28.1 1.5 %collective-permute-start.11 = (bf16[512,256]{1,0:T(8,128)(2,1)S(1)}, bf16[512,256]{1,0:T(8,128)(2,1)S(1)}, u32[]{:S(2)}, u32[]{:S(2)}) collective-permute-start(bf16[512,256]{1,0:T(8,128)(2,1)S(1)} %collective-permute-done.9.refs_8_), channel_id=1, source_target_pairs={{0,16},{4,20},{8,24},{12,28},{16,0},{20,4},{24,8},{28,12},{1,17},{... | collective-permute-start | bytes 786440 | tf_op jit(solution)/shard_map/ppermute | solution.py:27
  30.3 5.4 %collective-permute-done.10.refs_9_ = bf16[512,256]{1,0:T(8,128)(2,1)S(1)} collective-permute-done((bf16[512,256]{1,0:T(8,128)(2,1)S(1)}, bf16[512,256]{1,0:T(8,128)(2,1)S(1)}, u32[]{:S(2)}, u32[]{:S(2)}) %collective-permute-start.10) | collective-permute-done | bytes 262176 | tf_op jit(solution)/shard_map/ppermute | solution.py:27
  35.8 6.0 %collective-permute-done.11.refs_10_ = bf16[512,256]{1,0:T(8,128)(2,1)S(1)} collective-permute-done((bf16[512,256]{1,0:T(8,128)(2,1)S(1)}, bf16[512,256]{1,0:T(8,128)(2,1)S(1)}, u32[]{:S(2)}, u32[]{:S(2)}) %collective-permute-start.11) | collective-permute-done | bytes 262176 | tf_op jit(solution)/shard_map/ppermute | solution.py:27
  41.7 2.0 %collective-permute-start.15 = (bf16[512,256]{1,0:T(8,128)(2,1)S(1)}, bf16[512,256]{1,0:T(8,128)(2,1)}, u32[]{:S(2)}, u32[]{:S(2)}) collective-permute-start(bf16[512,256]{1,0:T(8,128)(2,1)S(1)} %collective-permute-done.11.refs_10_), channel_id=1, source_target_pairs={{0,1},{1,0},{2,3},{3,2},{4,5},{5,4},{6,7},{7,6},{8,9},{9,8},{10,11... | collective-permute-start | bytes 786440 | tf_op jit(solution)/shard_map/ppermute | solution.py:27
  43.8 6.7 %plane1_12.1.refs_4_ = f32[2,2,256,256]{3,2,1,0:T(8,128)S(1)} custom-call(bf16[2,3,256,256]{3,2,1,0:T(8,128)(2,1)S(1)} %bitcast.74, f32[3,3,3,2,2,256]{5,4,3,2,1,0:T(2,128)S(1)} %bitcast.77, f32[2,2,3,2,2,256]{5,4,3,2,1,0:T(2,128)S(1)} %pad_maximum_fusion.refs_2_.refs_3_), custom_call_target="tpu_custom_call" | custom-call | flops 3221225472 | bytes 4194304 | tf_op jit(solution)/shard_map/plane1_12/pallas_call | solution.py:166
  51.8 8.3 %plane0_120.1.refs_4_ = f32[2,2,256,256]{3,2,1,0:T(8,128)S(1)} custom-call(bf16[2,3,256,256]{3,2,1,0:T(8,128)(2,1)S(1)} %bitcast.73, bf16[2,3,256,256]{3,2,1,0:T(8,128)(2,1)S(1)} %bitcast.75, f32[3,3,3,2,2,256]{5,4,3,2,1,0:T(2,128)S(1)} %bitcast.78, f32[2,2,3,2,2,256]{5,4,3,2,1,0:T(2,128)S(1)} %pad_maximum_fusion.refs_2_.refs_3_, ...), custom_call_target="tpu_custom_call" | custom-call | flops 4026531840 | bytes 4194304 | tf_op jit(solution)/shard_map/plane0_120/pallas_call | solution.py:166
  60.7 5.5 %plane1_0.1 = (bf16[128,256]{1,0:T(8,128)(2,1)S(1)}, bf16[128,256]{1,0:T(8,128)(2,1)S(1)}, bf16[128,256]{1,0:T(8,128)(2,1)S(1)}, bf16[128,256]{1,0:T(8,128)(2,1)...) custom-call(bf16[2,3,256,256]{3,2,1,0:T(8,128)(2,1)S(1)} %bitcast.76, ...), custom_call_target="tpu_custom_call" | custom-call | flops 2415919104 | bytes 4194304 | tf_op jit(solution)/shard_map/plane1_0/pallas_call | solution.py:166
  66.2 0.7 copy-done
  67.4 0.7 copy-done.2
  68.1 0.7 copy-done.4
  69.8 0.8 collective-permute-start.4
  70.7 3.6 %collective-permute-done.3.refs_2_ = bf16[128,256]{1,0:T(8,128)(2,1)S(1)} collective-permute-done((bf16[128,256]{1,0:T(8,128)(2,1)S(1)}, bf16[128,256]{1,0:T(8,128)(2,1)S(1)}, u32[]{:S(2)}, u32[]{:S(2)}) %collective-permute-start.3) | collective-permute-done | bytes 65568 | tf_op jit(solution)/shard_map/ppermute | solution.py:27
  74.2 4.7 %collective-permute-start.5 = (bf16[128,256]{1,0:T(8,128)(2,1)S(1)}, bf16[128,256]{1,0:T(8,128)(2,1)S(1)}, u32[]{:S(2)}, u32[]{:S(2)}) collective-permute-start(bf16[128,256]{1,0:T(8,128)(2,1)S(1)} %get-tuple-element.17), channel_id=1, source_target_pairs={{0,16},{4,20},{8,24},{12,28},{16,0},{20,4},{24,8},{28,12},{1,17},{... | collective-permute-start | bytes 196616 | tf_op jit(solution)/shard_map/ppermute | solution.py:27
  79.1 2.1 %collective-permute-done.5.refs_4_ = bf16[128,256]{1,0:T(8,128)(2,1)S(1)} collective-permute-done((bf16[128,256]{1,0:T(8,128)(2,1)S(1)}, bf16[128,256]{1,0:T(8,128)(2,1)S(1)}, u32[]{:S(2)}, u32[]{:S(2)}) %collective-permute-start.5) | collective-permute-done | bytes 65568 | tf_op jit(solution)/shard_map/ppermute | solution.py:27
  81.2 1.0 %collective-permute-start.7 = (bf16[128,256]{1,0:T(8,128)(2,1)}, bf16[128,256]{1,0:T(8,128)(2,1)S(1)}, u32[]{:S(2)}, u32[]{:S(2)}) collective-permute-start(bf16[128,256]{1,0:T(8,128)(2,1)} %get-tuple-element.19), channel_id=1, source_target_pairs={{0,24},{4,28},{8,16},{12,20},{16,8},{20,12},{24,0},{28,4},{1,25},{... | collective-permute-start | bytes 196616 | tf_op jit(solution)/shard_map/ppermute | solution.py:27
  82.6 1.9 %collective-permute-start.8 = (bf16[128,256]{1,0:T(8,128)(2,1)S(1)}, bf16[128,256]{1,0:T(8,128)(2,1)S(1)}, u32[]{:S(2)}, u32[]{:S(2)}) collective-permute-start(bf16[128,256]{1,0:T(8,128)(2,1)S(1)} %get-tuple-element.20), channel_id=1, source_target_pairs={{0,28},{4,24},{8,20},{12,16},{16,12},{20,8},{24,4},{28,0},{1,29},{... | collective-permute-start | bytes 196616 | tf_op jit(solution)/shard_map/ppermute | solution.py:27
  84.6 2.0 %collective-permute-done.7.refs_6_ = bf16[128,256]{1,0:T(8,128)(2,1)S(1)} collective-permute-done((bf16[128,256]{1,0:T(8,128)(2,1)}, bf16[128,256]{1,0:T(8,128)(2,1)S(1)}, u32[]{:S(2)}, u32[]{:S(2)}) %collective-permute-start.7) | collective-permute-done | bytes 65568 | tf_op jit(solution)/shard_map/ppermute | solution.py:27
  86.6 1.2 %collective-permute-done.8.refs_7_ = bf16[128,256]{1,0:T(8,128)(2,1)S(1)} collective-permute-done((bf16[128,256]{1,0:T(8,128)(2,1)S(1)}, bf16[128,256]{1,0:T(8,128)(2,1)S(1)}, u32[]{:S(2)}, u32[]{:S(2)}) %collective-permute-start.8) | collective-permute-done | bytes 65568 | tf_op jit(solution)/shard_map/ppermute | solution.py:27
  87.9 0.9 %copy-done.1 = bf16[512,256]{1,0:T(8,128)(2,1)S(1)} copy-done((bf16[512,256]{1,0:T(8,128)(2,1)S(1)}, bf16[512,256]{1,0:T(8,128)(2,1)}, u32[]{:S(2)}) %copy-start.1) | copy-done | bytes 262168
  88.8 0.9 %copy-done.3 = bf16[512,256]{1,0:T(8,128)(2,1)S(1)} copy-done((bf16[512,256]{1,0:T(8,128)(2,1)S(1)}, bf16[512,256]{1,0:T(8,128)(2,1)}, u32[]{:S(2)}) %copy-start.3) | copy-done | bytes 262168
  89.8 0.9 %copy-done.5 = bf16[512,256]{1,0:T(8,128)(2,1)S(1)} copy-done((bf16[512,256]{1,0:T(8,128)(2,1)S(1)}, bf16[512,256]{1,0:T(8,128)(2,1)}, u32[]{:S(2)}) %copy-start.5) | copy-done | bytes 262168
  90.7 3.3 %quark_products.1 = f32[2,16,2,32,256]{4,3,2,1,0:T(8,128)} custom-call(s32[16]{0:T(128)S(1)} %stack.77.where_ref, bf16[128,256]{1,0:T(8,128)(2,1)S(1)} %get-tuple-element.13.refs_0_, bf16[128,256]{1,0:T(8,128)(2,1)S(1)} %collective-permute-done.2.refs_1_, bf16[128,256]{1,0:T(8,128)(2,1)S(1)} %collective-permute-done.3.refs_2_, ...), custom_call_target="tpu_custom_call" | custom-call | flops 536870912 | bytes 7340032 | tf_op jit(solution)/shard_map/quark_products/pallas_call | solution.py:302
  (84 shorter events, 7.4 us)
Async XLA Ops:
  1.7 14.3 %collective-permute-start.1 = (s32[30]{0:T(128)S(1)}, s32[30]{0:T(128)S(1)}, u32[]{:S(2)}, u32[]{:S(2)}) collective-permute-start(s32[30]{0:T(128)S(1)} %pad_add_fusion), channel_id=1, source_target_pairs={{0,1},{1,0},{2,3},{3,2},{4,5},{5,4},{6,7},{7,6},{8,9},{9,8},{10,11... | collective-permute-start | bytes 368 | tf_op jit(solution)/shard_map/ppermute | solution.py:22
  9.1 6.4 %copy-start.10 = (s32[4]{0:T(128)S(1)}, s32[4]{0:T(128)}, u32[]{:S(2)}) copy-start(s32[4]{0:T(128)} %param.11) | copy-start | bytes 52
  9.3 50.8 %collective-permute-start = (bf16[2,3,256,256]{3,2,1,0:T(8,128)(2,1)S(1)}, bf16[2,3,256,256]{3,2,1,0:T(8,128)(2,1)}, u32[]{:S(2)}, u32[]{:S(2)}) collective-permute-start(bf16[2,3,256,256]{3,2,1,0:T(8,128)(2,1)S(1)} %bitcast.72), channel_id=1, source_target_pairs={{0,28},{4,0},{8,4},{12,8},{16,12},{20,16},{24,20},{28,24},{1,29},{... | collective-permute-start | bytes 2359304 | tf_op jit(solution)/shard_map/ppermute | solution.py:22
  12.1 4.3 %copy-start.8 = (s32[2,3]{1,0:T(2,128)S(1)}, s32[2,3]{1,0:T(2,128)}, u32[]{:S(2)}) copy-start(s32[2,3]{1,0:T(2,128)} %param.9) | copy-start | bytes 76
  12.9 17.2 %copy-start.9 = (f32[2]{0:T(128)S(1)}, f32[2]{0:T(128)}, u32[]{:S(2)}) copy-start(f32[2]{0:T(128)} %constant.119.clone) | copy-start | bytes 28
  12.9 30.9 %copy-start.6 = (f32[1,3,3,3,2,2,256]{6,5,4,3,2,1,0:T(2,128)S(1)}, f32[1,3,3,3,2,2,256]{6,5,4,3,2,1,0:T(2,128)}, u32[]{:S(2)}) copy-start(f32[1,3,3,3,2,2,256]{6,5,4,3,2,1,0:T(2,128)} %param.8) | copy-start | bytes 331780
  12.9 13.7 %collective-permute-start.9 = (bf16[512,256]{1,0:T(8,128)(2,1)}, bf16[512,256]{1,0:T(8,128)(2,1)S(1)}, u32[]{:S(2)}, u32[]{:S(2)}) collective-permute-start(bf16[512,256]{1,0:T(8,128)(2,1)} %reshape.356), channel_id=1, source_target_pairs={{0,2},{2,0},{1,3},{3,1},{4,6},{6,4},{5,7},{7,5},{8,10},{10,8},{9,1... | collective-permute-start | bytes 786440 | tf_op jit(solution)/shard_map/ppermute | solution.py:22
  26.6 9.2 %collective-permute-start.10 = (bf16[512,256]{1,0:T(8,128)(2,1)S(1)}, bf16[512,256]{1,0:T(8,128)(2,1)S(1)}, u32[]{:S(2)}, u32[]{:S(2)}) collective-permute-start(bf16[512,256]{1,0:T(8,128)(2,1)S(1)} %collective-permute-done.9.refs_8_), channel_id=1, source_target_pairs={{0,8},{4,12},{8,0},{12,4},{16,24},{20,28},{24,16},{28,20},{1,9},{5... | collective-permute-start | bytes 786440 | tf_op jit(solution)/shard_map/ppermute | solution.py:27
  28.1 13.6 %collective-permute-start.11 = (bf16[512,256]{1,0:T(8,128)(2,1)S(1)}, bf16[512,256]{1,0:T(8,128)(2,1)S(1)}, u32[]{:S(2)}, u32[]{:S(2)}) collective-permute-start(bf16[512,256]{1,0:T(8,128)(2,1)S(1)} %collective-permute-done.9.refs_8_), channel_id=1, source_target_pairs={{0,16},{4,20},{8,24},{12,28},{16,0},{20,4},{24,8},{28,12},{1,17},{... | collective-permute-start | bytes 786440 | tf_op jit(solution)/shard_map/ppermute | solution.py:27
  29.6 12.1 %collective-permute-start.12 = (bf16[512,256]{1,0:T(8,128)(2,1)S(1)}, bf16[512,256]{1,0:T(8,128)(2,1)S(1)}, u32[]{:S(2)}, u32[]{:S(2)}) collective-permute-start(bf16[512,256]{1,0:T(8,128)(2,1)S(1)} %collective-permute-done.9.refs_8_), channel_id=1, source_target_pairs={{0,24},{4,28},{8,16},{12,20},{16,8},{20,12},{24,0},{28,4},{1,25},{... | collective-permute-start | bytes 786440 | tf_op jit(solution)/shard_map/ppermute | solution.py:27
  30.2 20.3 %collective-permute-start.13 = (bf16[512,256]{1,0:T(8,128)(2,1)S(1)}, bf16[512,256]{1,0:T(8,128)(2,1)S(1)}, u32[]{:S(2)}, u32[]{:S(2)}) collective-permute-start(bf16[512,256]{1,0:T(8,128)(2,1)S(1)} %collective-permute-done.9.refs_8_), channel_id=1, source_target_pairs={{0,1},{1,0},{2,3},{3,2},{4,5},{5,4},{6,7},{7,6},{8,9},{9,8},{10,11... | collective-permute-start | bytes 786440 | tf_op jit(solution)/shard_map/ppermute | solution.py:27
  35.8 14.9 %collective-permute-start.17 = (bf16[512,256]{1,0:T(8,128)(2,1)S(1)}, bf16[512,256]{1,0:T(8,128)(2,1)S(1)}, u32[]{:S(2)}, u32[]{:S(2)}) collective-permute-start(bf16[512,256]{1,0:T(8,128)(2,1)S(1)} %collective-permute-done.9.refs_8_), channel_id=1, source_target_pairs={{0,4},{4,0},{8,12},{12,8},{16,20},{20,16},{24,28},{28,24},{1,5},{5... | collective-permute-start | bytes 786440 | tf_op jit(solution)/shard_map/ppermute | solution.py:27
  41.7 9.4 %collective-permute-start.14 = (bf16[512,256]{1,0:T(8,128)(2,1)S(1)}, bf16[512,256]{1,0:T(8,128)(2,1)S(1)}, u32[]{:S(2)}, u32[]{:S(2)}) collective-permute-start(bf16[512,256]{1,0:T(8,128)(2,1)S(1)} %collective-permute-done.10.refs_9_), channel_id=1, source_target_pairs={{0,1},{1,0},{2,3},{3,2},{4,5},{5,4},{6,7},{7,6},{8,9},{9,8},{10,11... | collective-permute-start | bytes 786440 | tf_op jit(solution)/shard_map/ppermute | solution.py:27
  41.7 10.0 %collective-permute-start.15 = (bf16[512,256]{1,0:T(8,128)(2,1)S(1)}, bf16[512,256]{1,0:T(8,128)(2,1)}, u32[]{:S(2)}, u32[]{:S(2)}) collective-permute-start(bf16[512,256]{1,0:T(8,128)(2,1)S(1)} %collective-permute-done.11.refs_10_), channel_id=1, source_target_pairs={{0,1},{1,0},{2,3},{3,2},{4,5},{5,4},{6,7},{7,6},{8,9},{9,8},{10,11... | collective-permute-start | bytes 786440 | tf_op jit(solution)/shard_map/ppermute | solution.py:27
  50.5 10.1 %copy-start.7 = (f32[1,3,3,3,2,2,256]{6,5,4,3,2,1,0:T(2,128)S(1)}, f32[1,3,3,3,2,2,256]{6,5,4,3,2,1,0:T(2,128)}, u32[]{:S(2)}) copy-start(f32[1,3,3,3,2,2,256]{6,5,4,3,2,1,0:T(2,128)} %param.8) | copy-start | bytes 331780
  50.5 15.6 %collective-permute-start.18 = (bf16[512,256]{1,0:T(8,128)(2,1)S(1)}, bf16[512,256]{1,0:T(8,128)(2,1)S(1)}, u32[]{:S(2)}, u32[]{:S(2)}) collective-permute-start(bf16[512,256]{1,0:T(8,128)(2,1)S(1)} %collective-permute-done.10.refs_9_), channel_id=1, source_target_pairs={{0,4},{4,0},{8,12},{12,8},{16,20},{20,16},{24,28},{28,24},{1,5},{5... | collective-permute-start | bytes 786440 | tf_op jit(solution)/shard_map/ppermute | solution.py:27
  50.6 16.7 %collective-permute-start.19 = (bf16[512,256]{1,0:T(8,128)(2,1)S(1)}, bf16[512,256]{1,0:T(8,128)(2,1)S(1)}, u32[]{:S(2)}, u32[]{:S(2)}) collective-permute-start(bf16[512,256]{1,0:T(8,128)(2,1)S(1)} %collective-permute-done.11.refs_10_), channel_id=1, source_target_pairs={{0,4},{4,0},{8,12},{12,8},{16,20},{20,16},{24,28},{28,24},{1,5},{5... | collective-permute-start | bytes 786440 | tf_op jit(solution)/shard_map/ppermute | solution.py:27
  51.1 15.0 %collective-permute-start.16 = (bf16[512,256]{1,0:T(8,128)(2,1)S(1)}, bf16[512,256]{1,0:T(8,128)(2,1)}, u32[]{:S(2)}, u32[]{:S(2)}) collective-permute-start(bf16[512,256]{1,0:T(8,128)(2,1)S(1)} %collective-permute-done.12.refs_11_), channel_id=1, source_target_pairs={{0,1},{1,0},{2,3},{3,2},{4,5},{5,4},{6,7},{7,6},{8,9},{9,8},{10,11... | collective-permute-start | bytes 786440 | tf_op jit(solution)/shard_map/ppermute | solution.py:27
  51.8 16.3 %collective-permute-start.20 = (bf16[512,256]{1,0:T(8,128)(2,1)S(1)}, bf16[512,256]{1,0:T(8,128)(2,1)S(1)}, u32[]{:S(2)}, u32[]{:S(2)}) collective-permute-start(bf16[512,256]{1,0:T(8,128)(2,1)S(1)} %collective-permute-done.12.refs_11_), channel_id=1, source_target_pairs={{0,4},{4,0},{8,12},{12,8},{16,20},{20,16},{24,28},{28,24},{1,5},{5... | collective-permute-start | bytes 786440 | tf_op jit(solution)/shard_map/ppermute | solution.py:27
  60.1 9.2 %collective-permute-start.21 = (bf16[512,256]{1,0:T(8,128)(2,1)S(1)}, bf16[512,256]{1,0:T(8,128)(2,1)S(1)}, u32[]{:S(2)}, u32[]{:S(2)}) collective-permute-start(bf16[512,256]{1,0:T(8,128)(2,1)S(1)} %collective-permute-done.13.refs_12_), channel_id=1, source_target_pairs={{0,4},{4,0},{8,12},{12,8},{16,20},{20,16},{24,28},{28,24},{1,5},{5... | collective-permute-start | bytes 786440 | tf_op jit(solution)/shard_map/ppermute | solution.py:27
  66.1 3.7 %collective-permute-start.2 = (bf16[128,256]{1,0:T(8,128)(2,1)S(1)}, bf16[128,256]{1,0:T(8,128)(2,1)S(1)}, u32[]{:S(2)}, u32[]{:S(2)}) collective-permute-start(bf16[128,256]{1,0:T(8,128)(2,1)S(1)} %get-tuple-element.14), channel_id=1, source_target_pairs={{0,4},{4,0},{8,12},{12,8},{16,20},{20,16},{24,28},{28,24},{1,5},{5... | collective-permute-start | bytes 196616 | tf_op jit(solution)/shard_map/ppermute | solution.py:27
  66.9 21.0 %collective-permute-start.22 = (bf16[512,256]{1,0:T(8,128)(2,1)S(1)}, bf16[512,256]{1,0:T(8,128)(2,1)S(1)}, u32[]{:S(2)}, u32[]{:S(2)}) collective-permute-start(bf16[512,256]{1,0:T(8,128)(2,1)S(1)} %collective-permute-done.14.refs_13_), channel_id=1, source_target_pairs={{0,4},{4,0},{8,12},{12,8},{16,20},{20,16},{24,28},{28,24},{1,5},{5... | collective-permute-start | bytes 786440 | tf_op jit(solution)/shard_map/ppermute | solution.py:27
  68.1 19.8 %collective-permute-start.23 = (bf16[512,256]{1,0:T(8,128)(2,1)}, bf16[512,256]{1,0:T(8,128)(2,1)S(1)}, u32[]{:S(2)}, u32[]{:S(2)}) collective-permute-start(bf16[512,256]{1,0:T(8,128)(2,1)} %collective-permute-done.15.refs_14_), channel_id=1, source_target_pairs={{0,4},{4,0},{8,12},{12,8},{16,20},{20,16},{24,28},{28,24},{1,5},{5... | collective-permute-start | bytes 786440 | tf_op jit(solution)/shard_map/ppermute | solution.py:27
  68.8 19.1 %collective-permute-start.24 = (bf16[512,256]{1,0:T(8,128)(2,1)}, bf16[512,256]{1,0:T(8,128)(2,1)S(1)}, u32[]{:S(2)}, u32[]{:S(2)}) collective-permute-start(bf16[512,256]{1,0:T(8,128)(2,1)} %collective-permute-done.16.refs_15_), channel_id=1, source_target_pairs={{0,4},{4,0},{8,12},{12,8},{16,20},{20,16},{24,28},{28,24},{1,5},{5... | collective-permute-start | bytes 786440 | tf_op jit(solution)/shard_map/ppermute | solution.py:27
  69.3 5.0 %collective-permute-start.3 = (bf16[128,256]{1,0:T(8,128)(2,1)S(1)}, bf16[128,256]{1,0:T(8,128)(2,1)S(1)}, u32[]{:S(2)}, u32[]{:S(2)}) collective-permute-start(bf16[128,256]{1,0:T(8,128)(2,1)S(1)} %get-tuple-element.15), channel_id=1, source_target_pairs={{0,8},{4,12},{8,0},{12,4},{16,24},{20,28},{24,16},{28,20},{1,9},{5... | collective-permute-start | bytes 196616 | tf_op jit(solution)/shard_map/ppermute | solution.py:27
  69.8 9.1 %collective-permute-start.4 = (bf16[128,256]{1,0:T(8,128)(2,1)S(1)}, bf16[128,256]{1,0:T(8,128)(2,1)S(1)}, u32[]{:S(2)}, u32[]{:S(2)}) collective-permute-start(bf16[128,256]{1,0:T(8,128)(2,1)S(1)} %get-tuple-element.16), channel_id=1, source_target_pairs={{0,12},{4,8},{8,4},{12,0},{16,28},{20,24},{24,20},{28,16},{1,13},{... | collective-permute-start | bytes 196616 | tf_op jit(solution)/shard_map/ppermute | solution.py:27
  74.2 6.9 %collective-permute-start.5 = (bf16[128,256]{1,0:T(8,128)(2,1)S(1)}, bf16[128,256]{1,0:T(8,128)(2,1)S(1)}, u32[]{:S(2)}, u32[]{:S(2)}) collective-permute-start(bf16[128,256]{1,0:T(8,128)(2,1)S(1)} %get-tuple-element.17), channel_id=1, source_target_pairs={{0,16},{4,20},{8,24},{12,28},{16,0},{20,4},{24,8},{28,12},{1,17},{... | collective-permute-start | bytes 196616 | tf_op jit(solution)/shard_map/ppermute | solution.py:27
  78.9 3.7 %collective-permute-start.6 = (bf16[128,256]{1,0:T(8,128)(2,1)S(1)}, bf16[128,256]{1,0:T(8,128)(2,1)S(1)}, u32[]{:S(2)}, u32[]{:S(2)}) collective-permute-start(bf16[128,256]{1,0:T(8,128)(2,1)S(1)} %get-tuple-element.18), channel_id=1, source_target_pairs={{0,20},{4,16},{8,28},{12,24},{16,4},{20,0},{24,12},{28,8},{1,21},{... | collective-permute-start | bytes 196616 | tf_op jit(solution)/shard_map/ppermute | solution.py:27
  81.2 5.5 %collective-permute-start.7 = (bf16[128,256]{1,0:T(8,128)(2,1)}, bf16[128,256]{1,0:T(8,128)(2,1)S(1)}, u32[]{:S(2)}, u32[]{:S(2)}) collective-permute-start(bf16[128,256]{1,0:T(8,128)(2,1)} %get-tuple-element.19), channel_id=1, source_target_pairs={{0,24},{4,28},{8,16},{12,20},{16,8},{20,12},{24,0},{28,4},{1,25},{... | collective-permute-start | bytes 196616 | tf_op jit(solution)/shard_map/ppermute | solution.py:27
  82.6 5.2 %collective-permute-start.8 = (bf16[128,256]{1,0:T(8,128)(2,1)S(1)}, bf16[128,256]{1,0:T(8,128)(2,1)S(1)}, u32[]{:S(2)}, u32[]{:S(2)}) collective-permute-start(bf16[128,256]{1,0:T(8,128)(2,1)S(1)} %get-tuple-element.20), channel_id=1, source_target_pairs={{0,28},{4,24},{8,20},{12,16},{16,12},{20,8},{24,4},{28,0},{1,29},{... | collective-permute-start | bytes 196616 | tf_op jit(solution)/shard_map/ppermute | solution.py:27
  87.9 1.0 %copy-start.1 = (bf16[512,256]{1,0:T(8,128)(2,1)S(1)}, bf16[512,256]{1,0:T(8,128)(2,1)}, u32[]{:S(2)}) copy-start(bf16[512,256]{1,0:T(8,128)(2,1)} %copy-done) | copy-start | bytes 786436
  88.8 0.9 %copy-start.3 = (bf16[512,256]{1,0:T(8,128)(2,1)S(1)}, bf16[512,256]{1,0:T(8,128)(2,1)}, u32[]{:S(2)}) copy-start(bf16[512,256]{1,0:T(8,128)(2,1)} %copy-done.2) | copy-start | bytes 786436
  (4 other events, 3.0 us)

commit v2 on v1

--- a/solution.py
+++ b/solution.py
@@ -14,6 +14,7 @@
 SPINS = 16
 ROWS = 16
 HALF = 128
+VMEM_BYTES = 20 * 2**20
 
 
 def from_behind(value, axis, steps):
@@ -93,8 +94,7 @@
     next_ref = refs.pop(0) if 0 in dirs else None
     u_ref, phi_ref = refs.pop(0), refs.pop(0)
     part_ref = refs.pop(0) if has_part else None
-    where_ref = refs.pop(0) if n_out else None
-    out_refs = [refs.pop(0) for _ in range(n_out or 1)]
+    out_ref = refs.pop(0)
     g_ref, h_ref, sh_ref = refs[:3]
     n_h = phi_ref.shape[1]
     _, _, n_b, width = v_ref.shape
@@ -129,19 +129,19 @@
             if n_out:
                 refs[3][hel * 2 + part] = total
             else:
-                out_refs[0][hel, part] = total
+                out_ref[hel, part] = total
         return carry
 
     lax.fori_loop(0, n_h, multiply, 0)
     if n_out:
         own = n_b // n_out
-        for mask in range(n_out):
-            rows = pl.ds(pl.multiple_of((where_ref[0] ^ mask) * own, own), own)
+        for dev in range(n_out):
+            rows = pl.ds(dev * own, own)
             pieces = [refs[3][which, rows, :] for which in range(2 * n_h)]
-            out_refs[mask][...] = jnp.concatenate(pieces, 0).astype(jnp.bfloat16)
-
-
-def plane_call(plane, dirs, vec, ahead, link, phi, part=None, where=None, n_out=0):
+            out_ref[dev] = jnp.concatenate(pieces, 0).astype(jnp.bfloat16)
+
+
+def plane_call(plane, dirs, vec, ahead, link, phi, part=None, n_out=0):
     n_h = phi.shape[1]
     _, _, n_b, width = vec.shape
     vmem = pl.BlockSpec(memory_space=pltpu.VMEM)
@@ -154,22 +154,17 @@
         pltpu.VMEM((len(dirs), 2, 3, ROWS, width), jnp.float32),
     ]
     if n_out:
-        args.append(where)
-        specs.append(pl.BlockSpec(memory_space=pltpu.SMEM))
         scratch.append(pltpu.VMEM((2 * n_h, n_b, n_b), jnp.float32))
-        shape = jax.ShapeDtypeStruct((2 * n_h * (n_b // n_out), n_b), jnp.bfloat16)
-        out_shape = [shape] * n_out
-        out_specs = [vmem] * n_out
+        out_shape = jax.ShapeDtypeStruct((n_out, 2 * n_h * (n_b // n_out), n_b), jnp.bfloat16)
     else:
         out_shape = jax.ShapeDtypeStruct((n_h, 2, n_b, n_b), jnp.float32)
-        out_specs = vmem
     return pl.pallas_call(
         functools.partial(plane_kernel, plane, dirs, part is not None, n_out),
         in_specs=specs,
-        out_specs=out_specs,
+        out_specs=vmem,
         out_shape=out_shape,
         scratch_shapes=scratch,
-        compiler_params=pltpu.CompilerParams(vmem_limit_bytes=40 * 2**20),
+        compiler_params=pltpu.CompilerParams(vmem_limit_bytes=VMEM_BYTES),
         cost_estimate=pl.CostEstimate(
             flops=(16 + 8 * len(dirs)) * n_h * n_b * n_b * 3 * width,
             bytes_accessed=2**22,
@@ -179,18 +174,17 @@
     )(*args)
 
 
-def quark_kernel(n_got, n_tau, where_ref, *refs):
-    got_refs = refs[:n_got]
-    tau_refs = refs[n_got : n_got + n_tau]
-    out_ref, left_ref = refs[n_got + n_tau :]
+def quark_kernel(n_tau, where_ref, got_ref, *refs):
+    tau_refs = refs[:n_tau]
+    out_ref, left_ref = refs[n_tau:]
     n_h, n_pair, _, own, n_b = out_ref.shape
     row = lax.broadcasted_iota(jnp.int32, (n_b, 2 * n_b), 0)
     col = lax.broadcasted_iota(jnp.int32, (n_b, 2 * n_b), 1)
     even = (col == 2 * row).astype(jnp.bfloat16)
     odd = (col == 2 * row + 1).astype(jnp.bfloat16)
-    total = got_refs[0][...].astype(jnp.float32)
-    for ref in got_refs[1:]:
-        total = total + ref[...].astype(jnp.float32)
+    total = got_ref[0].astype(jnp.float32)
+    for dev in range(1, got_ref.shape[0]):
+        total = total + got_ref[dev].astype(jnp.float32)
     swap = []
     for hel in range(n_h):
         start = hel * 2 * own
@@ -221,28 +215,53 @@
                     out_ref[hel, pair, part] += res[start : start + own]
 
 
-def phases(momenta, weights, coord_x, n_x):
-    site = jnp.arange(LY * LZ, dtype=jnp.int32)
-    yy = site // LZ
-    zz = site % LZ
-    step = jnp.concatenate([jnp.zeros((1, 3), jnp.int32), jnp.eye(3, dtype=jnp.int32)], 0)
-    pos_x = coord_x[None, :, None] + step[:, 0, None, None]
-    pos_y = yy[None, None, :] + step[:, 1, None, None]
-    pos_z = zz[None, None, :] + step[:, 2, None, None]
-    mom = momenta[:, :, None, None, None]
-    part_x = (mom[:, 0] * pos_x % n_x).astype(jnp.float32) / n_x
-    part_y = (mom[:, 1] * pos_y % LY).astype(jnp.float32) / LY
-    part_z = (mom[:, 2] * pos_z % LZ).astype(jnp.float32) / LZ
-    theta = 2.0 * math.pi * (part_x + part_y + part_z)
-    wave = jnp.stack([jnp.cos(theta), -jnp.sin(theta)], 1)
-    wts = weights[:, :, :, None, None, None]
-    here = 0.0
-    ahead = 0.0
-    sign = jnp.array([1.0, -1.0], jnp.float32)[None, None, :, None, None]
-    for k in range(momenta.shape[0]):
-        here = here + wts[:, k] * wave[k, :, 0][None, None]
-        ahead = ahead + wts[:, k] * jnp.swapaxes(wave[k, :, 1:], 0, 1)[None]
-    return jnp.stack([here, ahead * sign], 0)
+def phase_kernel(n_op, n_x, planes, *refs):
+    mom_refs = refs[:n_op]
+    num_refs = refs[n_op : 2 * n_op]
+    den_ref, where_ref, out_ref = refs[2 * n_op :]
+    _, n_h, _, _, _, width = out_ref.shape
+    n_mom = mom_refs[0].shape[0]
+    moms = [(op, k) for op in range(n_op) for k in range(n_mom)]
+    scale = 1.0 / math.sqrt(3.0 * n_x * LY * LZ)
+    shape = (planes * len(moms), width)
+    row = lax.broadcasted_iota(jnp.int32, shape, 0)
+    lane = lax.broadcasted_iota(jnp.int32, shape, 1)
+    yy = lane // LZ
+    zz = lane & (LZ - 1)
+
+    def spread(values):
+        res = jnp.full(shape, values[0], jnp.int32)
+        for which in range(1, len(values)):
+            res = jnp.where(row == which, values[which], res)
+        return res
+
+    comps = [[mom_refs[op][k, axis] for _ in range(planes) for op, k in moms] for axis in range(3)]
+    mom_x, mom_y, mom_z = [spread(comp) for comp in comps]
+    pos_x = where_ref[0] * planes + row // len(moms)
+    steps = ((0, 0, 0), (1, 0, 0), (0, 1, 0), (0, 0, 1))
+    waves = []
+    for step_x, step_y, step_z in steps:
+        turn_x = lax.rem(mom_x * (pos_x + step_x), n_x).astype(jnp.float32) * (1.0 / n_x)
+        turn_y = ((mom_y * (yy + step_y)) & (LY - 1)).astype(jnp.float32) * (1.0 / LY)
+        turn_z = ((mom_z * (zz + step_z)) & (LZ - 1)).astype(jnp.float32) * (1.0 / LZ)
+        turn = turn_x + turn_y + turn_z
+        theta = (2.0 * math.pi) * (turn - jnp.floor(turn))
+        waves.append((jnp.cos(theta), jnp.sin(theta)))
+    for hel in range(n_h):
+        which_h = where_ref[1] * n_h + hel
+        den = jnp.full((1, width), den_ref[which_h], jnp.int32).astype(jnp.float32)
+        for direc in range(NDIR):
+            wts = []
+            for op, k in moms:
+                num = num_refs[op][direc, k, which_h]
+                wts.append(jnp.full((1, width), num, jnp.int32).astype(jnp.float32) / den * scale)
+            for kind, wave in ((0, waves[0]), (1, waves[1 + direc])):
+                for plane in range(planes):
+                    start = plane * len(moms)
+                    real = sum(wt * wave[0][start + at : start + at + 1] for at, wt in enumerate(wts))
+                    imag = sum(wt * wave[1][start + at : start + at + 1] for at, wt in enumerate(wts))
+                    out_ref[kind, hel, direc, 0, plane : plane + 1, :] = real
+                    out_ref[kind, hel, direc, 1, plane : plane + 1, :] = -imag if kind == 0 else imag
 
 
 def shards(eigvecs, links, momenta, coef_num, coef_den, peram):
@@ -262,55 +281,76 @@
     piece = lax.dynamic_slice(
         peram.reshape(n_b, SPINS, 2, n_b), (first % n_b, first // n_b, 0, 0), (depth, 1, 2, n_b)
     ).reshape(depth * 2, n_b)
-    piece = from_behind(piece, "tm", n_tm - 1)
-
-    vecs = [jnp.transpose(eigvecs[0, :, :, :, plane, :], (0, 2, 1, 3)) for plane in range(planes)]
+    own_piece = from_behind(piece, "tm", n_tm - 1)
+
+    eigvecs, piece = lax.optimization_barrier((eigvecs, piece))
+    vecs = [jnp.transpose(eigvecs[0, :, :, :, 0, :], (0, 2, 1, 3))]
     upper = from_behind(vecs[0], "space", -1)
-
-    held = [(piece, my_space, my_op)]
-    for mask in range(2, n_space, 2):
-        held.append((across(piece, "space", mask), my_space ^ mask, my_op))
-    for mask in range(1, n_op):
-        held += [(across(arr, "op", mask), place, oper ^ mask) for arr, place, oper in held[: n_space // 2]]
-    held += [(across(arr, "space", 1), place ^ 1, oper) for arr, place, oper in held]
-    tau = [arr for arr, _, _ in held]
-    tau_place = jnp.stack([place * n_op + oper for _, place, oper in held]).astype(jnp.int32)
-
-    small = jnp.concatenate([momenta.reshape(-1), coef_num.reshape(-1)])
-    parts = [small] + [from_behind(small, "op", shift) for shift in range(1, n_op)]
-    n_mom = momenta.shape[0]
-    moms = jnp.concatenate([part[: n_mom * 3].reshape(n_mom, 3) for part in parts], 0)
-    nums = jnp.concatenate(
-        [part[n_mom * 3 :].reshape(coef_num.shape) for part in parts], 1
-    )
-    weights = nums.astype(jnp.float32) / coef_den.astype(jnp.float32)[:, None, None]
-    scale = 1.0 / math.sqrt(3.0 * n_x * LY * LZ)
-    weights = lax.dynamic_slice_in_dim(weights, my_op * n_h, n_h, 0) * scale
-    coord_x = planes * my_space + jnp.arange(planes, dtype=jnp.int32)
-    phi = phases(moms, weights, coord_x, n_x)
+    for plane in range(1, planes):
+        vecs.append(jnp.transpose(eigvecs[0, :, :, :, plane, :], (0, 2, 1, 3)))
+
+    nums = jnp.transpose(coef_num, (2, 1, 0))
+    both = [(momenta, nums)]
+    both += [(across(momenta, "op", mask), across(nums, "op", mask)) for mask in range(1, n_op)]
+    where = jnp.stack([my_space, my_op]).astype(jnp.int32)
+    smem = pl.BlockSpec(memory_space=pltpu.SMEM)
+    vmem = pl.BlockSpec(memory_space=pltpu.VMEM)
+    phi = pl.pallas_call(
+        functools.partial(phase_kernel, n_op, n_x, planes),
+        in_specs=[smem] * (2 * n_op + 2),
+        out_specs=vmem,
+        out_shape=jax.ShapeDtypeStruct((2, n_h, NDIR, 2, planes, width), jnp.float32),
+        name="phases",
+    )(*[mom for mom, _ in both], *[num for _, num in both], coef_den, where)
 
     link = links[0]
     last = planes - 1
     partial = plane_call(last, (1, 2), vecs[last], None, link, phi)
+    own_piece, partial = lax.optimization_barrier((own_piece, partial))
+    held = [(own_piece, my_space, my_op)]
+    for mask in range(2, n_space, 2):
+        held.append((across(own_piece, "space", mask), my_space ^ mask, my_op))
+    beyond = [across(own_piece, "op", mask) for mask in range(1, n_op)]
     for plane in range(last):
         partial = plane_call(plane, (1, 2, 0), vecs[plane], vecs[plane + 1], link, phi, partial)
-    where = my_space.astype(jnp.int32).reshape(1)
-    sums = plane_call(last, (0,), vecs[last], upper, link, phi, partial, where, n_space)
-    got = [sums[0]] + [across(sums[mask], "space", mask) for mask in range(1, n_space)]
-
-    vmem = pl.BlockSpec(memory_space=pltpu.VMEM)
+    arrs = [arr for arr, _, _ in held]
+    near = arrs[:3]
+    *near, partial = lax.optimization_barrier((*near, partial))
+    arrs = near + arrs[3:]
+    tau = list(zip(arrs, [place for _, place, _ in held]))
+    forward = []
+    for at, (arr, place) in enumerate(tau[:3]):
+        for mask in range(1, n_op):
+            forward.append((beyond[mask - 1] if at == 0 else across(arr, "op", mask), place, my_op ^ mask))
+    sums = plane_call(last, (0,), vecs[last], upper, link, phi, partial, n_space)
+    rest = [arr for arr, _ in tau[3:]]
+    *rest, sums = lax.optimization_barrier((*rest, sums))
+    tau = tau[:3] + [(arr, place) for arr, (_, place) in zip(rest, tau[3:])]
+    for arr, place in tau[3:]:
+        for mask in range(1, n_op):
+            forward.append((across(arr, "op", mask), place, my_op ^ mask))
+    pieces = [(arr, place, my_op) for arr, place in tau]
+    pieces += [(across(arr, "space", 1), place ^ 1, my_op) for arr, place in tau]
+    got = lax.all_to_all(sums, "space", 0, 0, tiled=True)
+    far = [arr for arr, _, _ in forward]
+    *far, got = lax.optimization_barrier((*far, got))
+    for arr, (_, place, oper) in zip(far, forward):
+        pieces += [(arr, place, oper), (across(arr, "space", 1), place ^ 1, oper)]
+    tau_place = jnp.stack([place * n_op + oper for _, place, oper in pieces]).astype(jnp.int32)
+    tau = [arr for arr, _, _ in pieces]
+
     lines = pl.pallas_call(
-        functools.partial(quark_kernel, len(got), len(tau)),
-        in_specs=[pl.BlockSpec(memory_space=pltpu.SMEM)] + [vmem] * (len(got) + len(tau)),
+        functools.partial(quark_kernel, len(tau)),
+        in_specs=[smem, vmem] + [vmem] * len(tau),
         out_specs=vmem,
         out_shape=jax.ShapeDtypeStruct((n_h, SPINS, 2, own, n_b), jnp.float32),
         scratch_shapes=[pltpu.VMEM((n_h * 2 * own, 2 * n_b), jnp.bfloat16)],
-        compiler_params=pltpu.CompilerParams(vmem_limit_bytes=40 * 2**20),
+        compiler_params=pltpu.CompilerParams(vmem_limit_bytes=VMEM_BYTES),
         cost_estimate=pl.CostEstimate(
             flops=2 * SPINS * n_h * 2 * own * 2 * n_b * n_b, bytes_accessed=7 * 2**20, transcendentals=0
         ),
         name="quark_products",
-    )(tau_place, *got, *tau)
+    )(tau_place, got, *tau)
     return lines.reshape(1, n_h, 4, 4, 2, own, n_b)
 
 

time: 94.5 us -> 67.3 us (0.71)
  waiting for transfers between devices: 30.1 us -> 14.2 us
  local copies, waits for them, and re-layouts: 14.4 us -> 5.03 us
  starting transfers between devices: 24.2 us -> 21.1 us
  Pallas kernels: 23.8 us -> 25.9 us
    ppermute x3 -> x2, waiting for transfers between devices: 8.63 us -> 0.01 us  [from_behind(): return lax.ppermute(value, axis, pairs)]
    ppermute x22 -> x17, waiting for transfers between devices: 21.5 us -> 14.2 us  [across(): return lax.ppermute(value, axis, pairs)]
    slice x8 -> x0, local copies, waits for them, and re-layouts: 5.13 us -> none  [the longest x1 4.4 us: shards(): eigvecs[0, :, :, :, plane, :]]
    unnamed x26 -> x9, local copies, waits for them, and re-layouts: 7.14 us -> 3.09 us
    all_to_all x0 -> x1, starting transfers between devices: none -> 3.5 us  [shards(): got = lax.all_to_all(sums, 'space', 0, 0, tiled=True)]
    ppermute x22 -> x17, starting transfers between devices: 16.9 us -> 13.5 us  [across(): return lax.ppermute(value, axis, pairs)]
    ppermute x3 -> x2, starting transfers between devices: 7.27 us -> 4.17 us  [from_behind(): return lax.ppermute(value, axis, pairs)]
    pallas_call x1 -> x2, Pallas kernels: 3.34 us -> 5.25 us  [the longest x1 3.57 us: shards(): pl.pallas_call(functools.partial(quark_kernel, len(tau)), in_specs=[smem,...]
  transfers between devices with their start and end apart: 25 -> 20, of which waited for: 9 -> 8; matrix products, arithmetic and copies ran while one was open for 10% -> 5% of each run, Pallas kernels for 22% -> 33%
where the time goes in v2:
time: 67.3 us; the launch traced here: 66.9 us
  Pallas kernels  25.9 us (38%)
  starting transfers between devices  21.1 us (31%)
  waiting for transfers between devices  14.2 us (21%)
  local copies, waits for them, and re-layouts  5.03 us (7%)
    pallas_call x3, Pallas kernels, plane_call(): pl.pallas_call(functools.partial(plane_kernel, plane, dirs, part is not N...  20.6 us
    ppermute x17, waiting for transfers between devices, across(): return lax.ppermute(value, axis, pairs)  14.2 us
    ppermute x17, starting transfers between devices, across(): return lax.ppermute(value, axis, pairs)  13.5 us
    ppermute x2, starting transfers between devices, from_behind(): return lax.ppermute(value, axis, pairs)  4.17 us
    pallas_call x1, Pallas kernels, shards(): pl.pallas_call(functools.partial(quark_kernel, len(tau)), in_specs=[smem,...  3.57 us
    all_to_all x1, starting transfers between devices, shards(): got = lax.all_to_all(sums, 'space', 0, 0, tiled=True)  3.5 us
    unnamed x9, local copies, waits for them, and re-layouts  3.09 us
    pallas_call x1, Pallas kernels, shards(): pl.pallas_call(functools.partial(phase_kernel, n_op, n_x, planes), in_spe...  1.68 us
  transfers between devices with their start and end apart: 20, of which 8 were waited for; matrix products, arithmetic and copies ran while one was open for 5% of the time, Pallas kernels for 33%

profile of v2, /device:TPU:0, one launch (start us, length us, event | category | flops | bytes accessed | tf_op | source)
XLA Modules:
  0.0 66.9 jit_solution(1776723573783866026)
XLA Ops:
  0.0 3.0 %collective-permute-start.1 = (s32[2,3]{1,0:T(2,128)}, s32[2,3]{1,0:T(2,128)S(1)}, u32[]{:S(2)}, u32[]{:S(2)}) collective-permute-start(s32[2,3]{1,0:T(2,128)} %refs_0_.1), channel_id=1, source_target_pairs={{0,1},{1,0},{2,3},{3,2},{4,5},{5,4},{6,7},{7,6},{8,9},{9,8},{10,11... | collective-permute-start | bytes 80 | tf_op jit(solution)/shard_map/ppermute | solution.py:28
  3.1 1.1 %dynamic-slice_bitcast_fusion = bf16[256,1,2,256]{3,2,0,1:T(2,128)(2,1)S(1)} fusion(bf16[256,16,2,256]{3,2,1,0:T(2,128)(2,1)} %bitcast.37, s32[]{:T(128)S(6)} %select_n.14), kind=kLoop, calls=%fused_computation.2 | loop fusion | bytes 524292
  4.3 3.1 %collective-permute-start = (bf16[512,256]{1,0:T(8,128)(2,1)S(1)}, bf16[512,256]{1,0:T(8,128)(2,1)S(1)}, u32[]{:S(2)}, u32[]{:S(2)}) collective-permute-start(bf16[512,256]{1,0:T(8,128)(2,1)S(1)} %reshape.10), channel_id=1, source_target_pairs={{0,2},{2,0},{1,3},{3,1},{4,6},{6,4},{5,7},{7,5},{8,10},{10,8},{9,1... | collective-permute-start | bytes 786440 | tf_op jit(solution)/shard_map/ppermute | solution.py:23
  7.4 1.6 %copy.8 = bf16[1,2,256,3,2,256]{5,2,3,1,4,0:T(8,128)(2,1)S(1)} copy(bf16[1,2,256,3,2,256]{5,4,3,2,1,0:T(2,128)(2,1)} %param.6) | data formatting | bytes 3145728 | tf_op jit(solution)/shard_map/optimization_barrier | solution.py:286
  9.1 1.1 %collective-permute-start.9 = (bf16[2,3,256,256]{3,2,1,0:T(8,128)(2,1)S(1)}, bf16[2,3,256,256]{3,2,1,0:T(8,128)(2,1)}, u32[]{:S(2)}, u32[]{:S(2)}) collective-permute-start(bf16[2,3,256,256]{3,2,1,0:T(8,128)(2,1)S(1)} %get-tuple-element.33.refs_0_), channel_id=1, source_target_pairs={{0,28},{4,0},{8,4},{12,8},{16,12},{20,16},{24,20},{28,24},{1,29},{... | collective-permute-start | bytes 2359304 | tf_op jit(solution)/shard_map/ppermute | solution.py:23
  10.2 0.6 pad_add_fusion.refs_5_
  10.8 0.6 copy-done.3
  11.4 0.6 copy-done.2
  12.0 1.7 %phases.1.refs_2_.refs_3_ = f32[2,2,3,2,2,256]{5,4,3,2,1,0:T(2,128)} custom-call(s32[2,3]{1,0:T(2,128)} %refs_0_.1, s32[2,3]{1,0:T(2,128)} %copy-done.3, s32[3,2,4]{2,1,0:T(2,128)} %bitcast.39, s32[3,2,4]{2,1,0:T(2,128)} %copy-done.2, s32[4]{0:T(128)} %refs_4_.1, s32[2]{0:T(128)} %pad_add_fusion.refs_5_), custom_call_target="tpu_custom_call" | custom-call | tf_op jit(solution)/shard_map/phases/pallas_call | solution.py:298
  13.7 0.8 %copy-done = f32[2,2,3,2,2,256]{5,4,3,2,1,0:T(2,128)S(1)} copy-done((f32[2,2,3,2,2,256]{5,4,3,2,1,0:T(2,128)S(1)}, f32[2,2,3,2,2,256]{5,4,3,2,1,0:T(2,128)}, u32[]{:S(2)}) %copy-start) | copy-done | bytes 49176
  14.5 6.7 %plane1_12.1.refs_4_ = f32[2,2,256,256]{3,2,1,0:T(8,128)S(1)} custom-call(bf16[2,3,256,256]{3,2,1,0:T(8,128)(2,1)S(1)} %get-tuple-element.34.refs_0_.refs_1_, f32[3,3,3,2,2,256]{5,4,3,2,1,0:T(2,128)S(1)} %bitcast.34, f32[2,2,3,2,2,256]{5,4,3,2,1,0:T(2,128)S(1)} %copy-done), custom_call_target="tpu_custom_call" | custom-call | flops 3221225472 | bytes 4194304 | tf_op jit(solution)/shard_map/plane1_12/pallas_call | solution.py:161
  21.2 1.5 %collective-permute-start.8 = (bf16[512,256]{1,0:T(8,128)(2,1)S(1)}, bf16[512,256]{1,0:T(8,128)(2,1)S(1)}, u32[]{:S(2)}, u32[]{:S(2)}) collective-permute-start(bf16[512,256]{1,0:T(8,128)(2,1)S(1)} %collective-permute-done.refs_0_), channel_id=1, source_target_pairs={{0,24},{4,28},{8,16},{12,20},{16,8},{20,12},{24,0},{28,4},{1,25},{... | collective-permute-start | bytes 786440 | tf_op jit(solution)/shard_map/ppermute | solution.py:28
  22.7 0.5 collective-permute-start.5
  23.2 1.6 %collective-permute-start.4 = (bf16[512,256]{1,0:T(8,128)(2,1)S(1)}, bf16[512,256]{1,0:T(8,128)(2,1)S(1)}, u32[]{:S(2)}, u32[]{:S(2)}) collective-permute-start(bf16[512,256]{1,0:T(8,128)(2,1)S(1)} %collective-permute-done.refs_0_), channel_id=1, source_target_pairs={{0,8},{4,12},{8,0},{12,4},{16,24},{20,28},{24,16},{28,20},{1,9},{5... | collective-permute-start | bytes 786440 | tf_op jit(solution)/shard_map/ppermute | solution.py:28
  24.8 1.6 %collective-permute-start.3 = (bf16[512,256]{1,0:T(8,128)(2,1)S(1)}, bf16[512,256]{1,0:T(8,128)(2,1)S(1)}, u32[]{:S(2)}, u32[]{:S(2)}) collective-permute-start(bf16[512,256]{1,0:T(8,128)(2,1)S(1)} %collective-permute-done.refs_0_), channel_id=1, source_target_pairs={{0,1},{1,0},{2,3},{3,2},{4,5},{5,4},{6,7},{7,6},{8,9},{9,8},{10,11... | collective-permute-start | bytes 786440 | tf_op jit(solution)/shard_map/ppermute | solution.py:28
  26.3 8.3 %plane0_120.1.refs_4_ = f32[2,2,256,256]{3,2,1,0:T(8,128)S(1)} custom-call(bf16[2,3,256,256]{3,2,1,0:T(8,128)(2,1)S(1)} %get-tuple-element.33.refs_0_, bf16[2,3,256,256]{3,2,1,0:T(8,128)(2,1)S(1)} %get-tuple-element.34.refs_0_.refs_1_, f32[3,3,3,2,2,256]{5,4,3,2,1,0:T(2,128)S(1)} %bitcast.35, f32[2,2,3,2,2,256]{5,4,3,2,1,0:T(2,128)S(1)} %copy-done, ...), custom_call_target="tpu_custom_call" | custom-call | flops 4026531840 | bytes 4194304 | tf_op jit(solution)/shard_map/plane0_120/pallas_call | solution.py:161
  34.6 0.8 %collective-permute-done.5.refs_2_ = bf16[512,256]{1,0:T(8,128)(2,1)S(1)} collective-permute-done((bf16[512,256]{1,0:T(8,128)(2,1)S(1)}, bf16[512,256]{1,0:T(8,128)(2,1)S(1)}, u32[]{:S(2)}, u32[]{:S(2)}) %collective-permute-start.5) | collective-permute-done | bytes 262176 | tf_op jit(solution)/shard_map/ppermute | solution.py:28
  35.6 1.6 %collective-permute-start.6 = (bf16[512,256]{1,0:T(8,128)(2,1)S(1)}, bf16[512,256]{1,0:T(8,128)(2,1)S(1)}, u32[]{:S(2)}, u32[]{:S(2)}) collective-permute-start(bf16[512,256]{1,0:T(8,128)(2,1)S(1)} %collective-permute-done.4.refs_1_), channel_id=1, source_target_pairs={{0,1},{1,0},{2,3},{3,2},{4,5},{5,4},{6,7},{7,6},{8,9},{9,8},{10,11... | collective-permute-start | bytes 786440 | tf_op jit(solution)/shard_map/ppermute | solution.py:28
  37.1 5.7 %plane1_0.1 = bf16[8,128,256]{2,1,0:T(8,128)(2,1)} custom-call(bf16[2,3,256,256]{3,2,1,0:T(8,128)(2,1)S(1)} %get-tuple-element.34.refs_0_.refs_1_, bf16[2,3,256,256]{3,2,1,0:T(8,128)(2,1)} %collective-permute-done.9.refs_1_, f32[3,3,3,2,2,256]{5,4,3,2,1,0:T(2,128)S(1)} %bitcast.36, f32[2,2,3,2,2,256]{5,4,3,2,1,0:T(2,128)S(1)} %copy-done, ...), custom_call_target="tpu_custom_call" | custom-call | flops 2415919104 | bytes 4194304 | tf_op jit(solution)/shard_map/plane1_0/pallas_call | solution.py:161
  42.8 3.5 %all-to-all-start = ((bf16[8,128,256]{2,1,0:T(8,128)(2,1)}), bf16[8,128,256]{2,1,0:T(8,128)(2,1)S(1)}, u32[]{:S(2)}, u32[]{:S(2)}) async-start(bf16[8,128,256]{2,1,0:T(8,128)(2,1)} %plane1_0.1), calls=%async_computation | async-start | bytes 1048576 | tf_op jit(solution)/shard_map/all_to_all | solution.py:334
  46.3 0.5 collective-permute-start.7
  46.8 1.6 %collective-permute-start.10 = (bf16[512,256]{1,0:T(8,128)(2,1)S(1)}, bf16[512,256]{1,0:T(8,128)(2,1)S(1)}, u32[]{:S(2)}, u32[]{:S(2)}) collective-permute-start(bf16[512,256]{1,0:T(8,128)(2,1)S(1)} %collective-permute-done.8.refs_3_), channel_id=1, source_target_pairs={{0,1},{1,0},{2,3},{3,2},{4,5},{5,4},{6,7},{7,6},{8,9},{9,8},{10,11... | collective-permute-start | bytes 786440 | tf_op jit(solution)/shard_map/ppermute | solution.py:28
  48.4 0.5 collective-permute-start.12
  49.0 6.5 %collective-permute-done.7.refs_12_ = bf16[512,256]{1,0:T(8,128)(2,1)S(1)} collective-permute-done((bf16[512,256]{1,0:T(8,128)(2,1)S(1)}, bf16[512,256]{1,0:T(8,128)(2,1)S(1)}, u32[]{:S(2)}, u32[]{:S(2)}) %collective-permute-start.7) | collective-permute-done | bytes 262176 | tf_op jit(solution)/shard_map/ppermute | solution.py:28
  55.5 5.0 %collective-permute-done.10.refs_14_ = bf16[512,256]{1,0:T(8,128)(2,1)S(1)} collective-permute-done((bf16[512,256]{1,0:T(8,128)(2,1)S(1)}, bf16[512,256]{1,0:T(8,128)(2,1)S(1)}, u32[]{:S(2)}, u32[]{:S(2)}) %collective-permute-start.10) | collective-permute-done | bytes 262176 | tf_op jit(solution)/shard_map/ppermute | solution.py:28
  60.6 0.5 collective-permute-start.16
  61.1 0.4 collective-permute-start.18
  61.7 0.5 collective-permute-done.15.refs_9_
  62.2 0.4 collective-permute-done.16.refs_11_
  62.6 0.4 collective-permute-done.17.refs_13_
  63.0 0.4 collective-permute-done.18.refs_15_
  63.3 3.6 %quark_products.1 = f32[2,16,2,32,256]{4,3,2,1,0:T(8,128)} custom-call(s32[16]{0:T(128)S(1)} %stack.76.where_ref, bf16[8,128,256]{2,1,0:T(8,128)(2,1)S(1)} %all-to-all-done.got_ref, bf16[512,256]{1,0:T(8,128)(2,1)S(1)} %collective-permute-done.refs_0_, bf16[512,256]{1,0:T(8,128)(2,1)S(1)} %collective-permute-done.4.refs_1_, ...), custom_call_target="tpu_custom_call" | custom-call | flops 536870912 | bytes 7340032 | tf_op jit(solution)/shard_map/quark_products/pallas_call | solution.py:342
  (27 shorter events, 0.6 us)
Async XLA Ops:
  0.0 10.8 %collective-permute-start.1 = (s32[2,3]{1,0:T(2,128)}, s32[2,3]{1,0:T(2,128)S(1)}, u32[]{:S(2)}, u32[]{:S(2)}) collective-permute-start(s32[2,3]{1,0:T(2,128)} %refs_0_.1), channel_id=1, source_target_pairs={{0,1},{1,0},{2,3},{3,2},{4,5},{5,4},{6,7},{7,6},{8,9},{9,8},{10,11... | collective-permute-start | bytes 80 | tf_op jit(solution)/shard_map/ppermute | solution.py:28
  3.0 7.8 %collective-permute-start.2 = (s32[3,2,4]{2,1,0:T(2,128)}, s32[3,2,4]{2,1,0:T(2,128)S(1)}, u32[]{:S(2)}, u32[]{:S(2)}) collective-permute-start(s32[3,2,4]{2,1,0:T(2,128)} %bitcast.38), channel_id=1, source_target_pairs={{0,1},{1,0},{2,3},{3,2},{4,5},{5,4},{6,7},{7,6},{8,9},{9,8},{10,11... | collective-permute-start | bytes 296 | tf_op jit(solution)/shard_map/ppermute | solution.py:28
  4.3 16.9 %collective-permute-start = (bf16[512,256]{1,0:T(8,128)(2,1)S(1)}, bf16[512,256]{1,0:T(8,128)(2,1)S(1)}, u32[]{:S(2)}, u32[]{:S(2)}) collective-permute-start(bf16[512,256]{1,0:T(8,128)(2,1)S(1)} %reshape.10), channel_id=1, source_target_pairs={{0,2},{2,0},{1,3},{3,1},{4,6},{6,4},{5,7},{7,5},{8,10},{10,8},{9,1... | collective-permute-start | bytes 786440 | tf_op jit(solution)/shard_map/ppermute | solution.py:23
  9.0 4.7 %copy-start.1 = (f32[1,3,3,3,2,2,256]{6,5,4,3,2,1,0:T(2,128)S(1)}, f32[1,3,3,3,2,2,256]{6,5,4,3,2,1,0:T(2,128)}, u32[]{:S(2)}) copy-start(f32[1,3,3,3,2,2,256]{6,5,4,3,2,1,0:T(2,128)} %param.7) | copy-start | bytes 331780
  9.1 28.0 %collective-permute-start.9 = (bf16[2,3,256,256]{3,2,1,0:T(8,128)(2,1)S(1)}, bf16[2,3,256,256]{3,2,1,0:T(8,128)(2,1)}, u32[]{:S(2)}, u32[]{:S(2)}) collective-permute-start(bf16[2,3,256,256]{3,2,1,0:T(8,128)(2,1)S(1)} %get-tuple-element.33.refs_0_), channel_id=1, source_target_pairs={{0,28},{4,0},{8,4},{12,8},{16,12},{20,16},{24,20},{28,24},{1,29},{... | collective-permute-start | bytes 2359304 | tf_op jit(solution)/shard_map/ppermute | solution.py:23
  10.8 0.6 copy-start.3
  11.4 0.6 copy-start.2
  13.7 0.8 %copy-start = (f32[2,2,3,2,2,256]{5,4,3,2,1,0:T(2,128)S(1)}, f32[2,2,3,2,2,256]{5,4,3,2,1,0:T(2,128)}, u32[]{:S(2)}) copy-start(f32[2,2,3,2,2,256]{5,4,3,2,1,0:T(2,128)} %phases.1.refs_2_.refs_3_) | copy-start | bytes 147460
  21.2 21.6 %collective-permute-start.8 = (bf16[512,256]{1,0:T(8,128)(2,1)S(1)}, bf16[512,256]{1,0:T(8,128)(2,1)S(1)}, u32[]{:S(2)}, u32[]{:S(2)}) collective-permute-start(bf16[512,256]{1,0:T(8,128)(2,1)S(1)} %collective-permute-done.refs_0_), channel_id=1, source_target_pairs={{0,24},{4,28},{8,16},{12,20},{16,8},{20,12},{24,0},{28,4},{1,25},{... | collective-permute-start | bytes 786440 | tf_op jit(solution)/shard_map/ppermute | solution.py:28
  22.7 12.8 %collective-permute-start.5 = (bf16[512,256]{1,0:T(8,128)(2,1)S(1)}, bf16[512,256]{1,0:T(8,128)(2,1)S(1)}, u32[]{:S(2)}, u32[]{:S(2)}) collective-permute-start(bf16[512,256]{1,0:T(8,128)(2,1)S(1)} %collective-permute-done.refs_0_), channel_id=1, source_target_pairs={{0,16},{4,20},{8,24},{12,28},{16,0},{20,4},{24,8},{28,12},{1,17},{... | collective-permute-start | bytes 786440 | tf_op jit(solution)/shard_map/ppermute | solution.py:28
  23.2 12.4 %collective-permute-start.4 = (bf16[512,256]{1,0:T(8,128)(2,1)S(1)}, bf16[512,256]{1,0:T(8,128)(2,1)S(1)}, u32[]{:S(2)}, u32[]{:S(2)}) collective-permute-start(bf16[512,256]{1,0:T(8,128)(2,1)S(1)} %collective-permute-done.refs_0_), channel_id=1, source_target_pairs={{0,8},{4,12},{8,0},{12,4},{16,24},{20,28},{24,16},{28,20},{1,9},{5... | collective-permute-start | bytes 786440 | tf_op jit(solution)/shard_map/ppermute | solution.py:28
  24.8 23.6 %collective-permute-start.3 = (bf16[512,256]{1,0:T(8,128)(2,1)S(1)}, bf16[512,256]{1,0:T(8,128)(2,1)S(1)}, u32[]{:S(2)}, u32[]{:S(2)}) collective-permute-start(bf16[512,256]{1,0:T(8,128)(2,1)S(1)} %collective-permute-done.refs_0_), channel_id=1, source_target_pairs={{0,1},{1,0},{2,3},{3,2},{4,5},{5,4},{6,7},{7,6},{8,9},{9,8},{10,11... | collective-permute-start | bytes 786440 | tf_op jit(solution)/shard_map/ppermute | solution.py:28
  35.6 13.4 %collective-permute-start.6 = (bf16[512,256]{1,0:T(8,128)(2,1)S(1)}, bf16[512,256]{1,0:T(8,128)(2,1)S(1)}, u32[]{:S(2)}, u32[]{:S(2)}) collective-permute-start(bf16[512,256]{1,0:T(8,128)(2,1)S(1)} %collective-permute-done.4.refs_1_), channel_id=1, source_target_pairs={{0,1},{1,0},{2,3},{3,2},{4,5},{5,4},{6,7},{7,6},{8,9},{9,8},{10,11... | collective-permute-start | bytes 786440 | tf_op jit(solution)/shard_map/ppermute | solution.py:28
  42.8 17.7 %all-to-all-start = ((bf16[8,128,256]{2,1,0:T(8,128)(2,1)}), bf16[8,128,256]{2,1,0:T(8,128)(2,1)S(1)}, u32[]{:S(2)}, u32[]{:S(2)}) async-start(bf16[8,128,256]{2,1,0:T(8,128)(2,1)} %plane1_0.1), calls=%async_computation | async-start | bytes 1048576 | tf_op jit(solution)/shard_map/all_to_all | solution.py:334
  46.3 9.2 %collective-permute-start.7 = (bf16[512,256]{1,0:T(8,128)(2,1)S(1)}, bf16[512,256]{1,0:T(8,128)(2,1)S(1)}, u32[]{:S(2)}, u32[]{:S(2)}) collective-permute-start(bf16[512,256]{1,0:T(8,128)(2,1)S(1)} %collective-permute-done.5.refs_2_), channel_id=1, source_target_pairs={{0,1},{1,0},{2,3},{3,2},{4,5},{5,4},{6,7},{7,6},{8,9},{9,8},{10,11... | collective-permute-start | bytes 786440 | tf_op jit(solution)/shard_map/ppermute | solution.py:28
  46.8 13.7 %collective-permute-start.10 = (bf16[512,256]{1,0:T(8,128)(2,1)S(1)}, bf16[512,256]{1,0:T(8,128)(2,1)S(1)}, u32[]{:S(2)}, u32[]{:S(2)}) collective-permute-start(bf16[512,256]{1,0:T(8,128)(2,1)S(1)} %collective-permute-done.8.refs_3_), channel_id=1, source_target_pairs={{0,1},{1,0},{2,3},{3,2},{4,5},{5,4},{6,7},{7,6},{8,9},{9,8},{10,11... | collective-permute-start | bytes 786440 | tf_op jit(solution)/shard_map/ppermute | solution.py:28
  48.4 12.2 %collective-permute-start.11 = (bf16[512,256]{1,0:T(8,128)(2,1)S(1)}, bf16[512,256]{1,0:T(8,128)(2,1)S(1)}, u32[]{:S(2)}, u32[]{:S(2)}) collective-permute-start(bf16[512,256]{1,0:T(8,128)(2,1)S(1)} %collective-permute-done.refs_0_), channel_id=1, source_target_pairs={{0,4},{4,0},{8,12},{12,8},{16,20},{20,16},{24,28},{28,24},{1,5},{5... | collective-permute-start | bytes 786440 | tf_op jit(solution)/shard_map/ppermute | solution.py:28
  48.4 12.7 %collective-permute-start.12 = (bf16[512,256]{1,0:T(8,128)(2,1)S(1)}, bf16[512,256]{1,0:T(8,128)(2,1)S(1)}, u32[]{:S(2)}, u32[]{:S(2)}) collective-permute-start(bf16[512,256]{1,0:T(8,128)(2,1)S(1)} %collective-permute-done.4.refs_1_), channel_id=1, source_target_pairs={{0,4},{4,0},{8,12},{12,8},{16,20},{20,16},{24,28},{28,24},{1,5},{5... | collective-permute-start | bytes 786440 | tf_op jit(solution)/shard_map/ppermute | solution.py:28
  48.9 12.2 %collective-permute-start.13 = (bf16[512,256]{1,0:T(8,128)(2,1)S(1)}, bf16[512,256]{1,0:T(8,128)(2,1)S(1)}, u32[]{:S(2)}, u32[]{:S(2)}) collective-permute-start(bf16[512,256]{1,0:T(8,128)(2,1)S(1)} %collective-permute-done.5.refs_2_), channel_id=1, source_target_pairs={{0,4},{4,0},{8,12},{12,8},{16,20},{20,16},{24,28},{28,24},{1,5},{5... | collective-permute-start | bytes 786440 | tf_op jit(solution)/shard_map/ppermute | solution.py:28
  55.5 6.2 %collective-permute-start.14 = (bf16[512,256]{1,0:T(8,128)(2,1)S(1)}, bf16[512,256]{1,0:T(8,128)(2,1)}, u32[]{:S(2)}, u32[]{:S(2)}) collective-permute-start(bf16[512,256]{1,0:T(8,128)(2,1)S(1)} %collective-permute-done.8.refs_3_), channel_id=1, source_target_pairs={{0,4},{4,0},{8,12},{12,8},{16,20},{20,16},{24,28},{28,24},{1,5},{5... | collective-permute-start | bytes 786440 | tf_op jit(solution)/shard_map/ppermute | solution.py:28
  60.5 1.7 %collective-permute-start.15 = (bf16[512,256]{1,0:T(8,128)(2,1)S(1)}, bf16[512,256]{1,0:T(8,128)(2,1)}, u32[]{:S(2)}, u32[]{:S(2)}) collective-permute-start(bf16[512,256]{1,0:T(8,128)(2,1)S(1)} %collective-permute-done.3.refs_8_), channel_id=1, source_target_pairs={{0,4},{4,0},{8,12},{12,8},{16,20},{20,16},{24,28},{28,24},{1,5},{5... | collective-permute-start | bytes 786440 | tf_op jit(solution)/shard_map/ppermute | solution.py:28
  60.6 2.0 %collective-permute-start.16 = (bf16[512,256]{1,0:T(8,128)(2,1)S(1)}, bf16[512,256]{1,0:T(8,128)(2,1)}, u32[]{:S(2)}, u32[]{:S(2)}) collective-permute-start(bf16[512,256]{1,0:T(8,128)(2,1)S(1)} %collective-permute-done.6.refs_10_), channel_id=1, source_target_pairs={{0,4},{4,0},{8,12},{12,8},{16,20},{20,16},{24,28},{28,24},{1,5},{5... | collective-permute-start | bytes 786440 | tf_op jit(solution)/shard_map/ppermute | solution.py:28
  61.1 1.9 %collective-permute-start.17 = (bf16[512,256]{1,0:T(8,128)(2,1)S(1)}, bf16[512,256]{1,0:T(8,128)(2,1)}, u32[]{:S(2)}, u32[]{:S(2)}) collective-permute-start(bf16[512,256]{1,0:T(8,128)(2,1)S(1)} %collective-permute-done.7.refs_12_), channel_id=1, source_target_pairs={{0,4},{4,0},{8,12},{12,8},{16,20},{20,16},{24,28},{28,24},{1,5},{5... | collective-permute-start | bytes 786440 | tf_op jit(solution)/shard_map/ppermute | solution.py:28
  61.1 2.2 %collective-permute-start.18 = (bf16[512,256]{1,0:T(8,128)(2,1)S(1)}, bf16[512,256]{1,0:T(8,128)(2,1)}, u32[]{:S(2)}, u32[]{:S(2)}) collective-permute-start(bf16[512,256]{1,0:T(8,128)(2,1)S(1)} %collective-permute-done.10.refs_14_), channel_id=1, source_target_pairs={{0,4},{4,0},{8,12},{12,8},{16,20},{20,16},{24,28},{28,24},{1,5},{5... | collective-permute-start | bytes 786440 | tf_op jit(solution)/shard_map/ppermute | solution.py:28
